TPU v7x, 32 devices: a whole 2x2x4 slice. The times are simulated.
32 devices in a mesh: ctx: 16 (over z, y, core), tp: 2 (over x).
Axes of the slice: x: 2, y: 2, z: 4, core: 2. Of those that a mesh axis runs over, the one named last changes fastest.
Arguments:
- tokens: bfloat16 [8192, 1024], P('ctx'), may hold values from -6 to 6
- cotangent: bfloat16 [8192, 1024], P('ctx'), may hold values from -6 to 6
- block_order: int32 [16], replicated, may hold values from 0 to 15, each once
- segment_ids: int32 [1, 8192], replicated, may hold values from 0 to 3, as said below
- norm_gain: bfloat16 [1024], replicated, may hold values from 0.5 to 1.5
- w_query: bfloat16 [1024, 1024], P(None, 'tp'), may hold values from -0.1875 to 0.1875
- key_weight: bfloat16 [1024, 512], P(None, 'tp'), may hold values from -0.1875 to 0.1875
- value_weight: bfloat16 [1024, 512], P(None, 'tp'), may hold values from -0.1875 to 0.1875
- query_gain: bfloat16 [64], replicated, may hold values from 0.25 to 1.75
- key_gain: bfloat16 [64], replicated, may hold values from 0.25 to 1.75
- w_out: bfloat16 [1024, 1024], P('tp'), may hold values from -3 to 3
- ffn_gain: bfloat16 [1024], replicated, may hold values from 0.5 to 1.5
- w_gate: bfloat16 [1024, 4608], P(None, 'tp'), may hold values from -0.1875 to 0.1875
- w_up: bfloat16 [1024, 4608], P(None, 'tp'), may hold values from -0.1875 to 0.1875
- w_down: bfloat16 [4608, 1024], P('tp'), may hold values from -0.09375 to 0.09375
Outputs:
- output: bfloat16 [8192, 1024], P('ctx')
- input_grad: float32 [8192, 1024], P('ctx')
- grad_norm_gain: float32 [1024], replicated
- grad_w_query: float32 [1024, 1024], P(None, 'tp')
- grad_w_key: float32 [1024, 512], P(None, 'tp')
- grad_w_value: float32 [1024, 512], P(None, 'tp')
- grad_query_gain: float32 [64], replicated
- grad_key_gain: float32 [64], replicated
- grad_w_out: float32 [1024, 1024], P('tp')
- grad_ffn_gain: float32 [1024], replicated
- grad_w_gate: float32 [1024, 4608], P(None, 'tp')
- grad_w_up: float32 [1024, 4608], P(None, 'tp')
- grad_w_down: float32 [4608, 1024], P('tp')
Inputs may be any that keep to these rules, and one draw needn't show every extreme that they name: `block_order`: each index of ctx appears once. `segment_ids`: along each sequence the ids never fall; the first position has id 0 and the last id 3; document 0 covers more than the first three quarters of every sequence.
All inputs are finite; a program needn't handle non-finite values.
Results may differ from a plain program's by a relative error of at most 0.038.
Values may be sent and summed in bfloat16 or wider, within the bound.
No kernel may reach another device: no remote copies, remote signals or barrier semaphores. Data moves between devices by JAX's collectives and lax.ppermute only.
A program may use at most 576 MiB of HBM per device.

v0:
```python
import jax
import jax.numpy as jnp
from jax import lax
from jax.sharding import PartitionSpec as P

HEAD_SIZE = 64


EPSILON = 1e-05
ROPE_BASE = 1000000.0
MASKED = -1e30


def row_norm(value_rows, gain_vec):
    factor = lax.rsqrt(jnp.mean(value_rows * value_rows, axis=-1, keepdims=True) + EPSILON)
    return (value_rows * factor * gain_vec, factor)


def norm_back(upstream, value_rows, factor, gain_vec):
    inner_grad = upstream * gain_vec
    return factor * (
        inner_grad
        - value_rows * factor * factor * jnp.mean(inner_grad * value_rows, axis=-1, keepdims=True)
    )


def rotate(value_rows, cosine, sines):
    halfway = value_rows.shape[-1] // 2
    leading = value_rows[..., :halfway]
    trailing = value_rows[..., halfway:]
    return jnp.concatenate(
        [leading * cosine - trailing * sines, trailing * cosine + leading * sines], axis=-1
    )


def rotate_back(upstream, cosine, sines):
    halfway = upstream.shape[-1] // 2
    leading = upstream[..., :halfway]
    trailing = upstream[..., halfway:]
    return jnp.concatenate(
        [leading * cosine + trailing * sines, trailing * cosine - leading * sines], axis=-1
    )


def place_of(order_value, row_total, block_size, devices):
    local_row = jnp.arange(row_total, dtype=jnp.int32)
    block_start = jnp.where(
        local_row // block_size % 2 == 0, order_value, 2 * devices - 1 - order_value
    )
    return block_start * block_size + local_row % block_size


def masked_scores(query_block, key_block, query_place, key_place, query_seg, key_seg):
    raw_scores = (
        jnp.einsum("qhgd,khd->hgqk", query_block, key_block, preferred_element_type=jnp.float32)
        * 0.125
    )
    allowed = (key_place[None, :] <= query_place[:, None]) & (
        key_seg[None, :] == query_seg[:, None]
    )
    return jnp.where(allowed[None, None], raw_scores, MASKED)


def on_device(
    tokens,
    cotangent,
    block_order,
    segment_ids,
    norm_gain,
    w_query,
    key_weight,
    value_weight,
    query_gain,
    key_gain,
    w_out,
    ffn_gain,
    w_gate,
    w_up,
    w_down,
):
    devices = lax.axis_size("ctx")
    local_rows = tokens.shape[0]
    seq_count = segment_ids.shape[0]
    seq_span = local_rows // seq_count
    block_size = seq_span // 2
    pair_heads = key_weight.shape[1] // HEAD_SIZE
    query_heads = w_query.shape[1] // HEAD_SIZE
    group_size = query_heads // pair_heads
    own_place = place_of(block_order[lax.axis_index("ctx")], local_rows, block_size, devices)
    all_place = jax.vmap(
        lambda order_value: place_of(order_value, local_rows, block_size, devices)
    )(block_order)
    seq_rows = jnp.arange(local_rows, dtype=jnp.int32) // seq_span
    own_seg = segment_ids[seq_rows, own_place]
    all_seg = segment_ids[seq_rows[None, :], all_place]
    key_place = jnp.swapaxes(all_place.reshape(devices, seq_count, seq_span), 0, 1).reshape(
        seq_count, devices * seq_span
    )
    key_seg = jnp.swapaxes(all_seg.reshape(devices, seq_count, seq_span), 0, 1).reshape(
        seq_count, devices * seq_span
    )
    own_place_seq = own_place.reshape(seq_count, seq_span)
    own_seg_seq = own_seg.reshape(seq_count, seq_span)
    inverse = ROPE_BASE ** (-jnp.arange(0, HEAD_SIZE, 2, dtype=jnp.float32) / HEAD_SIZE)
    angles = own_place.astype(jnp.float32)[:, None] * inverse[None, :]
    cosine = jnp.cos(angles)[:, None, :]
    sines = jnp.sin(angles)[:, None, :]
    inputs = tokens.astype(jnp.float32)
    normed, scale_one = row_norm(inputs, norm_gain)
    hidden_input = normed.astype(jnp.bfloat16)
    query_raw = jnp.dot(hidden_input, w_query, preferred_element_type=jnp.float32).reshape(
        local_rows, query_heads, HEAD_SIZE
    )
    key_unnormed = jnp.dot(hidden_input, key_weight, preferred_element_type=jnp.float32).reshape(
        local_rows, pair_heads, HEAD_SIZE
    )
    value_unnormed = jnp.dot(hidden_input, value_weight, preferred_element_type=jnp.float32)
    query_norm, query_scale = row_norm(query_raw, query_gain)
    key_norm, key_scale = row_norm(key_unnormed, key_gain)
    queries = (
        rotate(query_norm, cosine, sines)
        .astype(jnp.bfloat16)
        .reshape(local_rows, pair_heads, group_size, HEAD_SIZE)
    )
    key_rows = (
        rotate(key_norm, cosine, sines)
        .astype(jnp.bfloat16)
        .reshape(local_rows, pair_heads * HEAD_SIZE)
    )
    value_rows = value_unnormed.astype(jnp.bfloat16)

    def sequence_keys(stacked, seq_index):
        return lax.dynamic_index_in_dim(stacked, seq_index, 1, keepdims=False).reshape(
            devices * seq_span, pair_heads, HEAD_SIZE
        )

    shared = (
        lax.all_gather(key_rows, "ctx", axis=0, tiled=True),
        lax.all_gather(value_rows, "ctx", axis=0, tiled=True),
    )
    key_all, value_all = tuple(
        (member.reshape(devices, seq_count, seq_span, pair_heads, HEAD_SIZE) for member in shared)
    )

    def forward_seq(seq_index):
        query_block = lax.dynamic_slice_in_dim(queries, seq_index * seq_span, seq_span, 0)
        key_block = sequence_keys(key_all, seq_index)
        value_block = sequence_keys(value_all, seq_index)
        scores = masked_scores(
            query_block,
            key_block,
            own_place_seq[seq_index],
            key_place[seq_index],
            own_seg_seq[seq_index],
            key_seg[seq_index],
        )
        peak_score = jnp.max(scores, axis=-1, keepdims=True)
        weights = jnp.exp(scores - peak_score)
        totals = jnp.sum(weights, axis=-1, keepdims=True)
        probabilities = (weights / totals).astype(jnp.bfloat16)
        result_block = jnp.einsum(
            "hgqk,khd->qhgd", probabilities, value_block, preferred_element_type=jnp.float32
        )
        return (result_block, (peak_score + jnp.log(totals))[..., 0])

    attended, log_total = lax.map(forward_seq, jnp.arange(seq_count, dtype=jnp.int32))
    attended_low = attended.reshape(local_rows, query_heads * HEAD_SIZE).astype(jnp.bfloat16)
    mixed = inputs + lax.psum(
        jnp.dot(attended_low, w_out, preferred_element_type=jnp.float32).astype(jnp.bfloat16), "tp"
    ).astype(jnp.float32)
    normed_two, scale_two = row_norm(mixed, ffn_gain)
    hidden_two = normed_two.astype(jnp.bfloat16)
    gating = jnp.dot(hidden_two, w_gate, preferred_element_type=jnp.float32)
    lifted = jnp.dot(hidden_two, w_up, preferred_element_type=jnp.float32)
    hidden_ffn = (jax.nn.silu(gating) * lifted).astype(jnp.bfloat16)
    result = mixed + lax.psum(
        jnp.dot(hidden_ffn, w_down, preferred_element_type=jnp.float32).astype(jnp.bfloat16), "tp"
    ).astype(jnp.float32)
    output = result.astype(jnp.bfloat16)
    grad_w_down = jnp.einsum("tf,td->fd", hidden_ffn, cotangent, preferred_element_type=jnp.float32)
    back_hidden = jnp.einsum("td,fd->tf", cotangent, w_down, preferred_element_type=jnp.float32)
    logistic = jax.nn.sigmoid(gating)
    back_gate = (back_hidden * lifted * logistic * (1.0 + gating * (1.0 - logistic))).astype(
        jnp.bfloat16
    )
    back_up = (back_hidden * gating * logistic).astype(jnp.bfloat16)
    grad_w_gate = jnp.einsum("td,tf->df", hidden_two, back_gate, preferred_element_type=jnp.float32)
    grad_w_up = jnp.einsum("td,tf->df", hidden_two, back_up, preferred_element_type=jnp.float32)
    back_part = jnp.einsum(
        "tf,df->td", back_gate, w_gate, preferred_element_type=jnp.float32
    ) + jnp.einsum("tf,df->td", back_up, w_up, preferred_element_type=jnp.float32)
    back_two = lax.psum(back_part.astype(jnp.bfloat16), "tp").astype(jnp.float32)
    grad_ffn_gain = jnp.sum(back_two * mixed * scale_two, axis=0)
    back_mixed = cotangent.astype(jnp.float32) + norm_back(back_two, mixed, scale_two, ffn_gain)
    back_proj = back_mixed.astype(jnp.bfloat16)
    grad_w_out = jnp.einsum(
        "ta,td->ad", attended_low, back_proj, preferred_element_type=jnp.float32
    )
    back_attn = (
        jnp.einsum("td,ad->ta", back_proj, w_out, preferred_element_type=jnp.float32)
        .astype(jnp.bfloat16)
        .reshape(local_rows, pair_heads, group_size, HEAD_SIZE)
    )
    key_back, value_back = (key_all, value_all)

    def query_side_seq(seq_index):
        query_block = lax.dynamic_slice_in_dim(queries, seq_index * seq_span, seq_span, 0)
        upstream_block = lax.dynamic_slice_in_dim(back_attn, seq_index * seq_span, seq_span, 0)
        key_block = sequence_keys(key_back, seq_index)
        value_block = sequence_keys(value_back, seq_index)
        scores = masked_scores(
            query_block,
            key_block,
            own_place_seq[seq_index],
            key_place[seq_index],
            own_seg_seq[seq_index],
            key_seg[seq_index],
        )
        probabilities = jnp.exp(scores - log_total[seq_index][..., None])
        back_probs = jnp.einsum(
            "qhgd,khd->hgqk", upstream_block, value_block, preferred_element_type=jnp.float32
        )
        row_delta = jnp.sum(back_probs * probabilities, axis=-1, keepdims=True)
        back_scores = (probabilities * (back_probs - row_delta)).astype(jnp.bfloat16)
        back_query = (
            jnp.einsum("hgqk,khd->qhgd", back_scores, key_block, preferred_element_type=jnp.float32)
            * 0.125
        )
        return (query_block, upstream_block, probabilities, back_scores, back_query, row_delta)

    def backward_seq(seq_index):
        query_block, upstream_block, probabilities, back_scores, back_query, row_delta = (
            query_side_seq(seq_index)
        )
        back_key = (
            jnp.einsum(
                "hgqk,qhgd->khd", back_scores, query_block, preferred_element_type=jnp.float32
            )
            * 0.125
        )
        back_value = jnp.einsum(
            "hgqk,qhgd->khd",
            probabilities.astype(jnp.bfloat16),
            upstream_block,
            preferred_element_type=jnp.float32,
        )
        return (back_query, back_key, back_value)

    back_query, back_key, back_value = lax.map(backward_seq, jnp.arange(seq_count, dtype=jnp.int32))

    def to_owners(stacked):
        return jnp.swapaxes(
            stacked.reshape(seq_count, devices, seq_span, pair_heads * HEAD_SIZE), 0, 1
        ).reshape(devices * local_rows, pair_heads * HEAD_SIZE)

    owner_key, owner_value = (
        lax.psum_scatter(
            to_owners(back_key).astype(jnp.bfloat16), "ctx", scatter_dimension=0, tiled=True
        ).astype(jnp.float32),
        lax.psum_scatter(
            to_owners(back_value).astype(jnp.bfloat16), "ctx", scatter_dimension=0, tiled=True
        ).astype(jnp.float32),
    )
    turned_query = rotate_back(
        back_query.reshape(local_rows, query_heads, HEAD_SIZE), cosine, sines
    )
    grad_query_part = jnp.sum(turned_query * query_raw * query_scale, axis=(0, 1))
    query_delta = (
        norm_back(turned_query, query_raw, query_scale, query_gain)
        .reshape(local_rows, query_heads * HEAD_SIZE)
        .astype(jnp.bfloat16)
    )
    turned_key = rotate_back(owner_key.reshape(local_rows, pair_heads, HEAD_SIZE), cosine, sines)
    grad_key_part = jnp.sum(turned_key * key_unnormed * key_scale, axis=(0, 1))
    key_delta = (
        norm_back(turned_key, key_unnormed, key_scale, key_gain)
        .reshape(local_rows, pair_heads * HEAD_SIZE)
        .astype(jnp.bfloat16)
    )
    value_delta = owner_value.astype(jnp.bfloat16)
    grad_w_query = jnp.einsum(
        "td,ta->da", hidden_input, query_delta, preferred_element_type=jnp.float32
    )
    grad_w_key = jnp.einsum(
        "td,ta->da", hidden_input, key_delta, preferred_element_type=jnp.float32
    )
    grad_w_value = jnp.einsum(
        "td,ta->da", hidden_input, value_delta, preferred_element_type=jnp.float32
    )
    one_part = jnp.einsum("ta,da->td", query_delta, w_query, preferred_element_type=jnp.float32)
    one_part = one_part + jnp.einsum(
        "ta,da->td", key_delta, key_weight, preferred_element_type=jnp.float32
    )
    one_part = one_part + jnp.einsum(
        "ta,da->td", value_delta, value_weight, preferred_element_type=jnp.float32
    )
    back_one, grad_query_gain, grad_key_gain = (
        lax.psum(one_part.astype(jnp.bfloat16), "tp").astype(jnp.float32),
        lax.psum(grad_query_part.astype(jnp.bfloat16), "tp").astype(jnp.float32),
        lax.psum(grad_key_part.astype(jnp.bfloat16), "tp").astype(jnp.float32),
    )
    grad_norm_gain = jnp.sum(back_one * inputs * scale_one, axis=0)
    input_grad = back_mixed + norm_back(back_one, inputs, scale_one, norm_gain)
    (
        grad_norm_gain,
        grad_w_query,
        grad_w_key,
        grad_w_value,
        grad_query_gain,
        grad_key_gain,
        grad_w_out,
        grad_ffn_gain,
        grad_w_gate,
        grad_w_up,
        grad_w_down,
    ) = (
        lax.psum(grad_norm_gain.astype(jnp.bfloat16), "ctx").astype(jnp.float32),
        lax.psum(grad_w_query.astype(jnp.bfloat16), "ctx").astype(jnp.float32),
        lax.psum(grad_w_key.astype(jnp.bfloat16), "ctx").astype(jnp.float32),
        lax.psum(grad_w_value.astype(jnp.bfloat16), "ctx").astype(jnp.float32),
        lax.psum(grad_query_gain.astype(jnp.bfloat16), "ctx").astype(jnp.float32),
        lax.psum(grad_key_gain.astype(jnp.bfloat16), "ctx").astype(jnp.float32),
        lax.psum(grad_w_out.astype(jnp.bfloat16), "ctx").astype(jnp.float32),
        lax.psum(grad_ffn_gain.astype(jnp.bfloat16), "ctx").astype(jnp.float32),
        lax.psum(grad_w_gate.astype(jnp.bfloat16), "ctx").astype(jnp.float32),
        lax.psum(grad_w_up.astype(jnp.bfloat16), "ctx").astype(jnp.float32),
        lax.psum(grad_w_down.astype(jnp.bfloat16), "ctx").astype(jnp.float32),
    )
    return (
        output,
        input_grad,
        grad_norm_gain,
        grad_w_query,
        grad_w_key,
        grad_w_value,
        grad_query_gain,
        grad_key_gain,
        grad_w_out,
        grad_ffn_gain,
        grad_w_gate,
        grad_w_up,
        grad_w_down,
    )


def solution(mesh):
    return jax.shard_map(
        on_device,
        mesh=mesh,
        in_specs=(
            P("ctx", None),
            P("ctx", None),
            P(),
            P(),
            P(),
            P(None, "tp"),
            P(None, "tp"),
            P(None, "tp"),
            P(),
            P(),
            P("tp", None),
            P(),
            P(None, "tp"),
            P(None, "tp"),
            P("tp", None),
        ),
        out_specs=(
            P("ctx", None),
            P("ctx", None),
            P(),
            P(None, "tp"),
            P(None, "tp"),
            P(None, "tp"),
            P(),
            P(),
            P("tp", None),
            P(),
            P(None, "tp"),
            P(None, "tp"),
            P("tp", None),
        ),
        check_vma=False,
    )
```

profile of v0, /device:TPU:0, one launch (start us, length us, event | category | flops | bytes accessed | tf_op | source)
XLA Modules:
  0.0 1123.0 jit_solution(15555849219566036286)
XLA Ops:
  19.9 4.1 gather_fusion.1
  24.0 48.0 %gather_fusion = s32[8192]{0:T(1024)S(1)} fusion(s32[1,8192]{1,0:T(1,128)S(1)} %copy-done.1, s32[8192]{0:T(1024)S(1)} %bitcast.164), kind=kCustom, calls=%fused_computation | custom fusion | bytes 131072 | tf_op jit(solution)/shard_map/gather | solution.py:95
  72.0 7.1 compare_and_fusion
  79.1 50.9 %fusion.81 = (f32[4,2,512]{2,1,0:T(2,128)S(1)}, f32[4,2,512,8192]{2,3,1,0:T(8,128)}) fusion(bf16[8192,4,64,1]{0,2,3,1:T(8,128)(2,1)} %bitcast.165, bf16[512,4,2,32]{0,3,2,1:T(8,128)(2,1)S(1)} %bitcast.179, bf16[512,4,2,32]{0,3,2,1:T(8,128)(2,1)S(1)} %bitcast.177, pred[512,8192]{0,1:T(8,128)(4,1)} %compare_and_fusion), kind=kOutput, calls=%fused_computation.178 | convolution fusion | flops 4396675072 | bytes 143147008 | tf_op jit(solution)/shard_map/while/body/eval_jaxpr/qhgd,khd->hgqk/dot_general | solution.py:55
  130.0 41.3 %fusion.3 = f32[4,2,512]{2,1,0:T(2,128)S(1)} fusion(f32[4,2,512,8192]{2,3,1,0:T(8,128)} %get-tuple-element.129, f32[4,2,512]{2,1,0:T(2,128)S(1)} %get-tuple-element.128), kind=kLoop, calls=%fused_computation.11 | loop fusion | flops 67104768 | bytes 134250496 | tf_op jit(solution)/shard_map/while/body/eval_jaxpr/reduce_sum | solution.py:159
  171.4 6.3 copy.39
  177.7 46.3 %fusion.33 = bf16[4,64,2,512]{3,1,2,0:T(8,128)(2,1)} fusion(bf16[8192,4,64,1]{0,2,3,1:T(8,128)(2,1)} %bitcast.171, f32[4,2,512,8192]{2,3,1,0:T(8,128)} %get-tuple-element.129, f32[4,2,512]{2,1,0:T(2,128)S(1)} %fusion.3, f32[4,2,512]{2,1,0:T(2,128)S(1)} %get-tuple-element.128), kind=kOutput, calls=%fused_computation.75 | convolution fusion | flops 4395892736 | bytes 138969088 | tf_op jit(solution)/shard_map/while/body/eval_jaxpr/hgqk,khd->qhgd/dot_general | solution.py:161
  228.4 41.2 %all-reduce.9.cloned.1.call-done = bf16[512,1024]{1,0:T(8,128)(2,1)} async-done(((bf16[512,1024]{1,0:T(8,128)(2,1)}), bf16[512,1024]{1,0:T(8,128)(2,1)}) %all-reduce.9.cloned.1.call-update) | async-done | bytes 1048592 | tf_op jit(solution)/shard_map/psum | solution.py:168
  271.9 5.5 fusion.82
  277.5 4.2 fusion.83
  281.8 7.9 multiply_convert_fusion.1
  292.4 3.6 add_convert_fusion.1
  296.3 7.0 convolution_convert_fusion.1
  303.3 5.9 convolution_convert_fusion.3
  309.2 27.0 %all-reduce.11.cloned.1.call-done = bf16[512,1024]{1,0:T(8,128)(2,1)} async-done(((bf16[512,1024]{1,0:T(8,128)(2,1)}), bf16[512,1024]{1,0:T(8,128)(2,1)}) %all-reduce.11.cloned.1.call-update) | async-done | bytes 1048592 | tf_op jit(solution)/shard_map/psum | solution.py:192
  341.3 86.5 %fusion = (f32[4,2,512]{2,1,0:T(2,128)S(1)}, f32[4,8192,512,2]{2,1,3,0:T(8,128)}) fusion(f32[4,2,512,8192]{2,3,1,0:T(8,128)} %get-tuple-element.129, f32[4,2,512]{2,1,0:T(2,128)S(1)} %bitcast.182, bf16[8192,4,64,1]{0,2,3,1:T(8,128)(2,1)} %bitcast.172, bf16[512,4,2,64]{0,3,2,1:T(8,128)(2,1)} %bitcast.173), kind=kOutput, calls=%fused_computation.4 | convolution fusion | flops 4395626496 | bytes 273186816 | tf_op jit(solution)/shard_map/while/body/eval_jaxpr/qhgd,khd->hgqk/dot_general | solution.py:220
  427.8 104.4 %fusion.2 = bf16[4,2,512,8192]{2,3,1,0:T(8,128)(2,1)} fusion(f32[4,8192,512,2]{2,1,3,0:T(8,128)} %get-tuple-element.131, f32[4,2,512,8192]{2,3,1,0:T(8,128)} %get-tuple-element.129, f32[4,2,512]{2,1,0:T(2,128)S(1)} %get-tuple-element.130, f32[4,2,512]{2,1,0:T(2,128)S(1)} %bitcast.183), kind=kLoop, calls=%fused_computation.6 | loop fusion | flops 134217728 | bytes 335577088 | tf_op jit(solution)/shard_map/while/body/eval_jaxpr/convert_element_type | solution.py:224
  532.2 29.7 %multiply_convert_fusion = bf16[4,64,8192]{2,1,0:T(8,128)(2,1)} fusion(bf16[4,2,512,8192]{2,3,1,0:T(8,128)(2,1)} %fusion.2, bf16[512,4,2,32]{0,3,2,1:T(8,128)(2,1)S(1)} %bitcast.180, bf16[512,4,2,32]{0,3,2,1:T(8,128)(2,1)S(1)} %bitcast.178), kind=kOutput, calls=%fused_computation.20 | convolution fusion | flops 4300210176 | bytes 71827456 | tf_op jit(solution)/shard_map/while/body/eval_jaxpr/hgqk,qhgd->khd/dot_general | solution.py:236
  562.9 47.5 %fusion.12 = bf16[4,64,8192]{2,1,0:T(8,128)(2,1)} fusion(bf16[512,4,2,64]{0,3,2,1:T(8,128)(2,1)S(1)} %bitcast.174, f32[4,2,512,8192]{2,3,1,0:T(8,128)} %get-tuple-element.129, f32[4,2,512]{2,1,0:T(2,128)S(1)} %bitcast.184), kind=kOutput, calls=%fused_computation.19 | convolution fusion | flops 4364173312 | bytes 138952704 | tf_op jit(solution)/shard_map/while/body/eval_jaxpr/hgqk,qhgd->khd/dot_general | solution.py:241
  610.4 25.0 %convolution_multiply_fusion = f32[4,64,2,512]{3,1,2,0:T(8,128)S(1)} fusion(bf16[8192,4,64,1]{0,2,3,1:T(8,128)(2,1)} %bitcast.166, bf16[4,2,512,8192]{2,3,1,0:T(8,128)(2,1)} %fusion.2), kind=kOutput, calls=%fused_computation.67 | convolution fusion | flops 4295229440 | bytes 72351744 | tf_op jit(solution)/shard_map/while/body/eval_jaxpr/hgqk,khd->qhgd/dot_general | solution.py:226
  643.6 67.1 %reduce-scatter.5.cloned.1.call-done = bf16[512,256]{0,1:T(8,128)(2,1)} async-done(((bf16[8192,256]{0,1:T(8,128)(2,1)}), bf16[512,256]{0,1:T(8,128)(2,1)}) %reduce-scatter.5.cloned.1.call-update) | async-done | bytes 262160 | tf_op jit(solution)/shard_map/reduce_scatter | solution.py:260
  710.7 3.3 add_convert_fusion
  714.2 7.0 convolution_convert_fusion.2
  721.3 4.3 convolution_convert_fusion
  733.3 5.0 all-reduce.2
  738.3 38.1 %all-reduce.15.cloned.1.call-done = (bf16[512,1024]{1,0:T(8,128)(2,1)}, bf16[512,1024]{1,0:T(8,128)(2,1)}) async-done(((bf16[512,1024]{1,0:T(8,128)(2,1)}, bf16[512,1024]{1,0:T(8,128)(2,1)}), (bf16[512,1024]{1,0:T(8,128)(2,1)}, bf16[512,1024]{1,0:T(8,128)(2,1)})) %all-reduce.15.cloned.1.call-update) | async-done | bytes 2097168 | tf_op jit(solution)/shard_map/psum | solution.py:176
  778.5 35.6 %all-reduce = (bf16[1024]{0:T(1024)(128)(2,1)S(1)}, bf16[64]{0:T(256)(128)(2,1)S(1)}, bf16[64]{0:T(256)(128)(2,1)S(1)}, bf16[1024]{0:T(1024)(128)(2,1)S(1)}) all-reduce(bf16[1024]{0:T(1024)(128)(2,1)S(1)} %get-tuple-element.71, bf16[64]{0:T(256)(128)(2,1)S(1)} %get-tuple-element.97, ...), channel_id=1, replica_groups=mesh['ctx'=16,'tp'=2] {'ctx'}, use_global_device_ids=true, to_apply=%region_18.19 | all-reduce | flops 2176 | bytes 8704 | tf_op jit(solution)/shard_map/psum | solution.py:317
  816.3 4.6 fusion.23
  820.9 273.1 %all-reduce.13.cloned.1.call-done = (bf16[1024,512]{1,0:T(8,128)(2,1)}, bf16[1024,256]{1,0:T(8,128)(2,1)}, bf16[1024,256]{1,0:T(8,128)(2,1)}, bf16[512,1024]{1,0...) async-done(((bf16[1024,512]{1,0:T(8,128)(2,1)}, bf16[1024,256]{1,0:T(8,128)(2,1)}, bf16[1024,256]{1,0:T(8,128)(2,1)}, ...) | async-done | bytes 17301520 | tf_op jit(solution)/shard_map/psum | solution.py:318
  1094.0 7.3 convert_element_type.261
  1101.3 4.4 convert_element_type.263
  1105.8 4.9 convert_element_type.265
  (252 shorter events, 52.6 us)
Async XLA Ops:
  7.2 10.5 copy-start
  7.2 71.9 %all-gather.5.cloned.1.call-start = ((), (), s32[]{:S(2)}) async-start(), calls=%async_computation.3 | async-start | bytes 4456448 | tf_op jit(solution)/shard_map/all_gather | solution.py:138
  8.9 8.8 copy-start.47
  9.6 8.1 copy-start.43
  14.9 156.4 %all-gather.3.cloned.1.call-start = ((), (), s32[]{:S(2)}) async-start(), calls=%async_computation.2 | async-start | bytes 4456448 | tf_op jit(solution)/shard_map/all_gather | solution.py:139
  16.3 253.4 %all-reduce.9.cloned.1.call-start = ((), (), s32[]{:S(2)}) async-start(), calls=%async_computation.4 | async-start | bytes 2097152 | tf_op jit(solution)/shard_map/psum | solution.py:168
  19.7 59.4 %copy-start.21 = (bf16[512,8,32]{0,2,1:T(8,128)(2,1)}, bf16[512,8,32]{0,2,1:T(8,128)(2,1)S(1)}, u32[]{:S(2)}) copy-start(bf16[512,8,32]{0,2,1:T(8,128)(2,1)S(1)} %get-tuple-element.110) | copy-start | bytes 786436
  19.7 59.4 %copy-start.23 = (bf16[512,8,32]{0,2,1:T(8,128)(2,1)}, bf16[512,8,32]{0,2,1:T(8,128)(2,1)S(1)}, u32[]{:S(2)}) copy-start(bf16[512,8,32]{0,2,1:T(8,128)(2,1)S(1)} %get-tuple-element.111) | copy-start | bytes 786436
  177.7 46.3 %copy-start.64 = (bf16[512,1024]{1,0:T(8,128)(2,1)S(1)}, bf16[512,1024]{1,0:T(8,128)(2,1)}, u32[]{:S(2)}) copy-start(bf16[512,1024]{1,0:T(8,128)(2,1)} %param.25) | copy-start | bytes 3145732
  224.0 45.7 %copy-start.3 = (bf16[512,1024]{1,0:T(8,128)(2,1)S(1)}, bf16[512,1024]{1,0:T(8,128)(2,1)}, u32[]{:S(2)}) copy-start(bf16[512,1024]{1,0:T(8,128)(2,1)} %param.15) | copy-start | bytes 3145732
  226.9 109.3 %all-reduce.11.cloned.1.call-start = ((), (), s32[]{:S(2)}) async-start(), calls=%async_computation.5 | async-start | bytes 2097152 | tf_op jit(solution)/shard_map/psum | solution.py:192
  227.2 111.9 %copy-start.41 = (f32[1024]{0:T(1024)}, f32[1024]{0:T(1024)S(1)}, u32[]{:S(2)}) copy-start(f32[1024]{0:T(1024)S(1)} %convert_element_type.219) | copy-start | bytes 12292
  271.4 67.7 %copy-start.45 = (f32[512]{0:T(512)}, f32[512]{0:T(512)S(1)}, u32[]{:S(2)}) copy-start(f32[512]{0:T(512)S(1)} %add_rsqrt_fusion.2) | copy-start | bytes 6148
  271.4 6.0 slice-start.4
  271.9 9.9 slice-start.6
  277.5 12.2 %slice-start.2 = ((s8[4718592]{0:T(1024)(128)(4,1)}), s8[4194304]{0:T(1024)(128)(4,1)S(1)}, s32[]{:S(2)}) async-start(s8[4718592]{0:T(1024)(128)(4,1)} %bitcast.189), calls=%async_computation.12 | async-start | bytes 8388608
  281.8 8.0 slice-start.3
  296.0 343.1 %reduce-scatter.3.cloned.1.call-start = ((), (), s32[]{:S(2)}) async-start(), calls=%async_computation.6 | async-start | bytes 4456448 | tf_op jit(solution)/shard_map/reduce_scatter | solution.py:257
  296.3 7.0 copy-start.69
  427.8 104.4 %copy-start.22 = (bf16[512,8,32]{0,2,1:T(8,128)(2,1)S(1)}, bf16[512,8,32]{0,2,1:T(8,128)(2,1)}, u32[]{:S(2)}) copy-start(bf16[512,8,32]{0,2,1:T(8,128)(2,1)} %copy-done.21) | copy-start | bytes 786436
  427.8 104.4 %copy-start.24 = (bf16[512,8,32]{0,2,1:T(8,128)(2,1)S(1)}, bf16[512,8,32]{0,2,1:T(8,128)(2,1)}, u32[]{:S(2)}) copy-start(bf16[512,8,32]{0,2,1:T(8,128)(2,1)} %copy-done.23) | copy-start | bytes 786436
  561.9 148.8 %reduce-scatter.5.cloned.1.call-start = ((), (), s32[]{:S(2)}) async-start(), calls=%async_computation.7 | async-start | bytes 4456448 | tf_op jit(solution)/shard_map/reduce_scatter | solution.py:260
  610.4 25.1 %copy-start.18 = (f32[512,32]{0,1:T(8,128)S(1)}, f32[512,32]{0,1:T(8,128)}, u32[]{:S(2)}) copy-start(f32[512,32]{0,1:T(8,128)} %copy-done.17) | copy-start | bytes 196612
  610.4 25.1 %copy-start.20 = (f32[512,32]{0,1:T(8,128)S(1)}, f32[512,32]{0,1:T(8,128)}, u32[]{:S(2)}) copy-start(f32[512,32]{0,1:T(8,128)} %copy-done.19) | copy-start | bytes 196612
  610.4 25.3 %copy-start.59 = (f32[64]{0:T(128)S(1)}, f32[64]{0:T(128)}, u32[]{:S(2)}) copy-start(f32[64]{0:T(128)} %copy-done.58) | copy-start | bytes 772
  610.4 166.0 %all-reduce.15.cloned.1.call-start = ((), (), s32[]{:S(2)}) async-start(), calls=%async_computation.9 | async-start | bytes 4194304 | tf_op jit(solution)/shard_map/psum | solution.py:176
  714.0 7.2 copy-start.27
  714.0 380.0 %all-reduce.13.cloned.1.call-start = ((), (), s32[]{:S(2)}) async-start(), calls=%async_computation.8 | async-start | bytes 34603008 | tf_op jit(solution)/shard_map/psum | solution.py:318
  714.2 7.0 copy-start.70
  733.1 45.4 %copy-start.52 = (bf16[1024]{0:T(1024)(128)(2,1)S(1)}, bf16[1024]{0:T(1024)(128)(2,1)}, u32[]{:S(2)}) copy-start(bf16[1024]{0:T(1024)(128)(2,1)} %get-tuple-element.69) | copy-start | bytes 6148
  1094.0 7.3 copy-start.10
  1094.0 11.8 %slice-start = ((s8[4718592]{0:T(1024)(128)(4,1)}), s8[4194304]{0:T(1024)(128)(4,1)S(1)}, s32[]{:S(2)}) async-start(s8[4718592]{0:T(1024)(128)(4,1)} %bitcast.175), calls=%async_computation.10 | async-start | bytes 8388608
  (55 other events, 169.1 us)
Sparse Core Ops, SparseCore 0:
  15.1 55.9 all-gather.4
  73.7 48.7 all-gather.2
  227.0 42.5 all-reduce.8
  296.1 40.0 all-reduce.10
  562.0 72.3 reduce-scatter.2
  639.2 71.4 reduce-scatter.4
  714.1 62.2 all-reduce.14
  784.0 309.8 all-reduce.12
where the time goes:
time: 1130 us; the launch traced here: 1120 us
  waiting for transfers between devices  447 us (40%)
  matrix products  356 us (32%)
  other arithmetic  198 us (18%)
  local copies, waits for them, and re-layouts  64 us (6%)
  blocking collectives  40.6 us (4%)
  between operations  16.2 us (1%)
    psum x1, waiting for transfers between devices, on_device(): lax.psum(grad_w_query.astype(jnp.bfloat16), 'ctx').astype(jnp.float32)  273 us
    convert_element_type x1, other arithmetic, query_side_seq(): (probabilities * (back_probs - row_delta)).astype(jnp.bfloat16)  104 us
    dot_general x1, matrix products, query_side_seq(): jnp.einsum('qhgd,khd->hgqk', upstream_block, value_block, preferred_eleme...  86.5 us
    reduce_scatter x1, waiting for transfers between devices, on_device(): lax.psum_scatter(to_owners(back_value).astype(jnp.bfloat16), 'ctx', scatt...  67.1 us
    dot_general x1, matrix products, masked_scores(): jnp.einsum('qhgd,khd->hgqk', query_block, key_block, preferred_element_ty...  50.9 us
    gather x1, local copies, waits for them, and re-layouts, on_device(): all_seg = segment_ids[seq_rows[None, :], all_place]  48 us
    dot_general x1, matrix products, backward_seq(): jnp.einsum('hgqk,qhgd->khd', probabilities.astype(jnp.bfloat16), upstream...  47.5 us
    dot_general x1, matrix products, forward_seq(): jnp.einsum('hgqk,khd->qhgd', probabilities, value_block, preferred_elemen...  46.3 us
  transfers between devices with their start and end apart: 8, of which 5 were waited for; matrix products, arithmetic and copies ran while one was open for 25% of the time, Pallas kernels for 0%

commit v1 on v0

v1 whole, which is shorter than its diff:
```python
import functools

import jax
import jax.numpy as jnp
import numpy as np
from jax import lax
from jax.experimental import pallas as pl
from jax.experimental.pallas import tpu as pltpu
from jax.sharding import PartitionSpec as P

HEAD_SIZE = 64
LANES = 2 * HEAD_SIZE
EPSILON = 1e-05
ROPE_BASE = 1000000.0
LOG2E = 1.4426950408889634
VMEM_BYTES = 56 * 2**20
f32, bf16 = jnp.float32, jnp.bfloat16
NT = (((1,), (1,)), ((), ()))


class Ring:
    def __init__(self, n_ctx):
        n = self.n = n_ctx // 2
        self.zs = 4 if n % 4 == 0 else n
        self.ys = n // self.zs
        order = [int(self.chip_at(np.int32(place))) for place in range(n)]
        self.to_right = [
            (order[i] * 2 + c, order[(i + 1) % n] * 2 + c) for i in range(n) for c in range(2)
        ]
        self.to_left = [(b, a) for a, b in self.to_right]
        self.to_sibling = [(i, i ^ 1) for i in range(n_ctx)]

    def chip_at(self, place):
        if self.ys == 1:
            return place
        where = np.where if isinstance(place, np.integer) else jnp.where
        turn = place - self.zs
        k, r = turn // (self.ys - 1), turn % (self.ys - 1)
        back = (self.zs - 1 - k) * self.ys + where(k % 2 == 0, 1 + r, self.ys - 1 - r)
        return where(place < self.zs, place * self.ys, back)

    def here(self):
        index = lax.axis_index("ctx")
        chip, core = index // 2, index % 2
        if self.ys == 1:
            return chip, core
        z, y = chip // self.ys, chip % self.ys
        k = self.zs - 1 - z
        back = self.zs + k * (self.ys - 1) + jnp.where(k % 2 == 0, y - 1, self.ys - 1 - y)
        return jnp.where(y == 0, z, back), core

    def distance(self, i):
        if isinstance(i, int):
            return -(i + 1) // 2 if i % 2 else i // 2
        return jnp.where(i % 2 == 1, -(i + 1) // 2, i // 2)

    def device_at(self, distance, other_core):
        place, core = self.here()
        return self.chip_at((place + distance + self.n) % self.n) * 2 + (core + other_core) % 2

    def right(self, x):
        return lax.ppermute(x, "ctx", self.to_right)

    def left(self, x):
        return lax.ppermute(x, "ctx", self.to_left)

    def sibling(self, x):
        return lax.ppermute(x, "ctx", self.to_sibling)


def total(*terms):
    out = terms[0].astype(f32)
    for term in terms[1:]:
        out = out + term.astype(f32)
    return out.astype(bf16)


def lower(x):
    return x[: x.shape[0] // 2]


def upper(x):
    return x[x.shape[0] // 2 :]


class RingSum:
    def __init__(self, ring):
        self.ring = ring
        self.h = ring.n // 2

    def far(self, terms):
        self.got_left = self.ring.right(total(*[lower(x) for x in terms]))
        self.got_right = self.ring.left(total(*[upper(x) for x in terms]))

    def step(self, d, terms_right, terms_left):
        if d == self.h - 1:
            a = jnp.concatenate(
                [
                    total(*[lower(x) for x in terms_right], self.got_left),
                    total(*[upper(x) for x in terms_right]),
                ]
            )
            b = jnp.concatenate(
                [
                    total(*[lower(x) for x in terms_left]),
                    total(*[upper(x) for x in terms_left], self.got_right),
                ]
            )
        else:
            a = total(*terms_right, self.got_left)
            b = total(*terms_left, self.got_right)
        self.got_left = self.ring.right(a)
        self.got_right = self.ring.left(b)
        return a, b

    def sums(self, terms):
        return total(*terms, self.got_left, self.got_right)


class RingGather:
    def __init__(self, ring, own):
        self.ring = ring
        self.parts = [own]
        self.r = self.l = own

    def step(self):
        ring = self.ring
        if len(self.parts) + 1 < ring.n:
            self.r = ring.right(self.r)
            self.l = ring.left(self.l)
            new = [self.r, self.l]
        else:
            new = [jnp.concatenate([ring.right(lower(self.r)), ring.left(upper(self.l))])]
        self.parts += new
        return new

    def all(self):
        while len(self.parts) < self.ring.n:
            self.step()
        return self.parts


def sum_over_ctx(ring, arrays):
    n = ring.n
    place, core = ring.here()
    outs = []
    for x in arrays:
        k = x.shape[0] // 2
        unit = k // n
        give = lax.dynamic_slice_in_dim(x, (1 - core) * k, k, 0)
        got = ring.sibling(give)
        keep = lax.dynamic_slice_in_dim(x, core * k, k, 0)

        def local(d):
            q = (place + d + n) % n
            return [lax.dynamic_slice_in_dim(y, q * unit, unit, 0) for y in (keep, got)]

        ring_sum = RingSum(ring)
        ring_sum.far(local(n // 2))
        for d in range(n // 2 - 1, 0, -1):
            ring_sum.step(d, local(d), local(-d))
        parts = RingGather(ring, ring_sum.sums(local(0))).all()
        out = jnp.zeros(x.shape, f32)
        for i, found in enumerate(parts):
            q = (place + ring.distance(i) + n) % n
            for c, part in ((core, found), (1 - core, ring.sibling(found))):
                out = lax.dynamic_update_slice_in_dim(
                    out, part.astype(f32), (c * n + q) * unit, 0
                )
        outs.append(out)
    return outs


def sum_over_pairs(x, axis, size):
    step = 1
    while step < size:
        x = x + lax.ppermute(x, axis, [(i, i ^ step) for i in range(size)])
        step *= 2
    return x


def sum_over_tp(x):
    size = lax.axis_size("tp")
    if size == 2:
        return x.astype(f32) + lax.ppermute(x, "tp", [(0, 1), (1, 0)]).astype(f32)
    return lax.psum(x, "tp").astype(f32)


class Tiles:
    def __init__(self, ring, first, count, seq_count, blk, order_ref, starts_ref):
        self.ring, self.first, self.slots = ring, first, 2 * count
        self.seq_count, self.blk = seq_count, blk
        self.order, self.starts = order_ref, starts_ref
        self.last = 4 * ring.n - 1
        self.rows = seq_count * (2 * self.slots + (first == 0))

    def start_of(self, seq, place):
        start = jnp.int32(0)
        for d in range(3):
            at = self.starts[seq, d]
            start = jnp.where(place >= at, at, start)
        return start

    def pair(self, row):
        seq, row = row % self.seq_count, row // self.seq_count
        slot, which = row // 2, row % 2
        if self.first == 0:
            both_high = slot == self.slots
            slot = jnp.where(both_high, 0, slot)
        mine = self.order[lax.axis_index("ctx")]
        source = self.ring.device_at(self.ring.distance(self.first + slot // 2), slot % 2)
        theirs = self.order[source]
        low = (which == 1) & (theirs <= mine)
        high = (which == 1) & (theirs > mine)
        if self.first == 0:
            low, high = low & jnp.logical_not(both_high), high | both_high
        q_place = jnp.where(low, mine, self.last - mine) * self.blk
        k_place = jnp.where(high, self.last - theirs, theirs) * self.blk
        q_tile = 2 * seq + jnp.where(low, 0, 1)
        k_tile = 2 * (self.seq_count * slot + seq) + jnp.where(high, 1, 0)
        k_end, q_end = k_place + self.blk - 1, q_place + self.blk - 1
        whole = (k_end <= q_place) & (k_place >= self.start_of(seq, q_end))
        empty = k_end < self.start_of(seq, q_place)
        kind = jnp.where(whole, 0, jnp.where(empty, 2, 1))
        return q_tile, k_tile, kind, (seq, q_place, k_place)

    def allowed(self, at, query_axis, shape):
        seq, q_place, k_place = at
        query = q_place + lax.broadcasted_iota(jnp.int32, shape, query_axis) % self.blk
        key = k_place + lax.broadcasted_iota(jnp.int32, shape, 1 - query_axis)
        return (key <= query) & (key >= self.start_of(seq, query))

    def run(self, tile):
        def body(row, carry):
            q_tile, k_tile, kind, at = self.pair(row)
            keys = pl.ds(pl.multiple_of(k_tile * self.blk, self.blk), self.blk)
            pl.when(kind == 0)(lambda: tile(q_tile, keys, None))
            pl.when(kind == 1)(lambda: tile(q_tile, keys, functools.partial(self.allowed, at)))
            return carry

        lax.fori_loop(0, self.rows, body, 0)


def forward_kernel(make, parts, heads, order_ref, starts_ref, q_ref, *refs):
    chunks, (acc_ref, out_ref, kv_ref) = refs[:parts], refs[parts:] if len(refs) == parts + 3 else (
        None,
        *refs[parts:],
    )
    tiles = make(order_ref, starts_ref)
    blk = tiles.blk
    first = lax.broadcasted_iota(jnp.int32, (blk, LANES), 1) < HEAD_SIZE
    for i, chunk in enumerate(chunks):
        kv_ref[i * chunk.shape[0] : (i + 1) * chunk.shape[0]] = chunk[...]
    out_ref[...] = jnp.zeros_like(out_ref) if acc_ref is None else acc_ref[...]

    def tile(q_tile, keys, mask):
        if mask is not None:
            allowed = mask(0, (q_ref.shape[2], blk))
        for h in range(heads):
            kv = kv_ref[keys, h * LANES : (h + 1) * LANES]
            scores = lax.dot_general(q_ref[h, q_tile], kv, NT, preferred_element_type=f32)
            weights = jnp.exp2(scores * LOG2E)
            if mask is not None:
                weights = jnp.where(allowed, weights, 0.0)
            one_v = jnp.where(first, jnp.ones_like(kv), kv)
            out_ref[h, q_tile] += jnp.dot(weights.astype(bf16), one_v, preferred_element_type=f32)

    tiles.run(tile)


def backward_kernel(
    make, parts, after, heads, order_ref, starts_ref, q_ref, do_ref, stat_ref, acc_ref, *refs
):
    chunks, refs = refs[:parts], refs[parts + after :]
    dq_ref, outs, (kv_ref, dkv_ref) = refs[0], refs[1:-2], refs[-2:]
    tiles = make(order_ref, starts_ref)
    blk = tiles.blk
    for i, chunk in enumerate(chunks):
        kv_ref[i * chunk.shape[0] : (i + 1) * chunk.shape[0]] = chunk[...]
    dq_ref[...] = acc_ref[...]
    dkv_ref[...] = jnp.zeros_like(dkv_ref)

    def tile(q_tile, keys, mask):
        if mask is not None:
            allowed = mask(1, (blk, q_ref.shape[2]))
        for h in range(heads):
            cols = slice(h * LANES, (h + 1) * LANES)
            kv = kv_ref[keys, cols]
            q = q_ref[h, q_tile]
            do = do_ref[h, q_tile]
            scores = lax.dot_general(kv, q, NT, preferred_element_type=f32)
            back_probs = lax.dot_general(kv, do, NT, preferred_element_type=f32)
            probs = jnp.exp2(scores * LOG2E - stat_ref[h, q_tile, 0:1])
            if mask is not None:
                probs = jnp.where(allowed, probs, 0.0)
            back_scores = (probs * (back_probs - stat_ref[h, q_tile, 1:2])).astype(bf16)
            both = jnp.concatenate([probs.astype(bf16), back_scores], axis=1)
            dkv_ref[keys, cols] += jnp.dot(
                both, jnp.concatenate([do, q], axis=0), preferred_element_type=f32
            )
            dq_ref[h, q_tile] += jnp.dot(kv.T[:HEAD_SIZE], back_scores, preferred_element_type=f32)

    tiles.run(tile)
    for i, out in enumerate(outs):
        out[...] = dkv_ref[i * out.shape[0] : (i + 1) * out.shape[0]].astype(out.dtype)


def in_smem():
    return pl.BlockSpec(memory_space=pltpu.SMEM)


def in_vmem():
    return pl.BlockSpec(memory_space=pltpu.VMEM)


def anywhere():
    return pl.BlockSpec(memory_space=pl.ANY)


class Attention:
    def __init__(self, ring, block_order, starts, blk):
        self.ring, self.order, self.starts = ring, block_order, starts
        self.blk, self.seq_count = blk, starts.shape[0]

    def _make(self, first, count):
        return lambda order_ref, starts_ref: Tiles(
            self.ring, first, count, self.seq_count, self.blk, order_ref, starts_ref
        )

    def _cost(self, first, count, heads, products, arrays):
        rows = self.seq_count * (4 * count + (first == 0))
        tile = 2 * self.blk * self.blk * heads * rows
        return pl.CostEstimate(
            flops=2 * tile * 256 * products,
            bytes_accessed=sum(x.size * x.dtype.itemsize for x in arrays),
            transcendentals=tile,
        )

    def forward(self, first, chunks, q, acc):
        heads, tiles, rows, _ = q.shape
        out = jax.ShapeDtypeStruct((heads, tiles, rows, LANES), f32)
        count = len(chunks) // 2
        held = [] if acc is None else [acc]
        keys, width = len(chunks) * chunks[0].shape[0], chunks[0].shape[1]
        return pl.pallas_call(
            functools.partial(forward_kernel, self._make(first, count), len(chunks), heads),
            out_shape=out,
            in_specs=[in_smem()] * 2 + [in_vmem()] * (1 + len(chunks) + len(held)),
            out_specs=in_vmem(),
            scratch_shapes=[pltpu.VMEM((keys, width), bf16)],
            compiler_params=pltpu.CompilerParams(vmem_limit_bytes=VMEM_BYTES),
            cost_estimate=self._cost(first, count, heads, 2, [q, *chunks, out, out]),
            name="attend_forward",
        )(self.order, self.starts, q, *chunks, *held)

    def backward(self, first, chunks, q, do, stats, acc, after):
        heads, tiles, rows, _ = q.shape
        count = len(chunks) // 2
        keys, width = len(chunks) * chunks[0].shape[0], chunks[0].shape[1]
        outs = [jax.ShapeDtypeStruct(acc.shape, f32)] + [
            jax.ShapeDtypeStruct(x.shape, bf16 if i % 2 else f32) for i, x in enumerate(chunks)
        ]
        dq, *grads = pl.pallas_call(
            functools.partial(
                backward_kernel, self._make(first, count), len(chunks), len(after), heads
            ),
            out_shape=outs,
            in_specs=[in_smem()] * 2
            + [in_vmem()] * (4 + len(chunks))
            + [anywhere()] * len(after),
            out_specs=[in_vmem()] * len(outs),
            scratch_shapes=[pltpu.VMEM((keys, width), bf16), pltpu.VMEM((keys, width), f32)],
            compiler_params=pltpu.CompilerParams(vmem_limit_bytes=VMEM_BYTES),
            cost_estimate=self._cost(first, count, heads, 5, [q, do, acc, *chunks, *outs]),
            name="attend_backward",
        )(self.order, self.starts, q, do, stats, acc, *chunks, *after)
        return dq, grads


def grads_kernel(ring, two_ref, gate_ref, up_ref, ffn_ref, cot_ref, keep_ref, give_ref, lhs_ref):
    _, core = ring.here()

    @pl.when(pl.program_id(0) == 0)
    def _():
        lhs_ref[...] = two_ref[...].T

    n = ring.n
    unit = lhs_ref.shape[0] // (2 * n)
    cols = gate_ref.shape[1]
    thin = cols // (2 * n)

    def store(at, value):
        rows = pl.ds(at, value.shape[1])

        @pl.when(core == 0)
        def _():
            keep_ref[:, rows] = value[:n]
            give_ref[:, rows] = value[n:]

        @pl.when(core == 1)
        def _():
            keep_ref[:, rows] = value[n:]
            give_ref[:, rows] = value[:n]

    for i, ref in enumerate((gate_ref, up_ref)):
        grad = jnp.dot(lhs_ref[...], ref[...], preferred_element_type=f32).astype(bf16)
        store(i * unit, grad.reshape(2 * n, unit, cols))
    down = jnp.dot(ffn_ref[...].T, cot_ref[...], preferred_element_type=f32).astype(bf16)
    down = down.reshape(2 * n, thin, down.shape[1])
    for q in range(down.shape[2] // cols):
        store(2 * unit + q * thin, down[:, :, q * cols : (q + 1) * cols])


def ffn_grads(ring, hidden_two, back_gate, back_up, hidden_ffn, cotangent):
    rows, width = hidden_two.shape
    units = back_gate.shape[1]
    n = ring.n
    wide = width // (2 * n) * 3
    cols = 256
    out = jax.ShapeDtypeStruct((n, wide, units), bf16)
    whole = pl.BlockSpec((rows, width), lambda j: (0, 0))
    block = pl.BlockSpec((rows, cols), lambda j: (0, j))
    cut = pl.BlockSpec((n, wide, cols), lambda j: (0, 0, j))
    return pl.pallas_call(
        functools.partial(grads_kernel, ring),
        grid=(units // cols,),
        out_shape=(out, out),
        in_specs=[whole, block, block, block, whole],
        out_specs=(cut, cut),
        scratch_shapes=[pltpu.VMEM((width, rows), bf16)],
        compiler_params=pltpu.CompilerParams(vmem_limit_bytes=VMEM_BYTES),
        cost_estimate=pl.CostEstimate(
            flops=6 * rows * width * units, bytes_accessed=20 * 2**20, transcendentals=0
        ),
        name="ffn_grads",
    )(hidden_two, back_gate, back_up, hidden_ffn, cotangent)


def place_kernel(ring, *refs):
    parts, (gate_ref, up_ref, down_ref) = refs[:-3], refs[-3:]
    place, core = ring.here()
    n = ring.n
    cols = gate_ref.shape[1]
    unit = gate_ref.shape[0] // (2 * n)
    thin = cols // (2 * n)
    for i, part in enumerate(parts):
        d = ring.distance(i // 2)
        q = (place + d + n) % n
        r = (core + i % 2) % 2 * n + q
        rows = pl.ds(pl.multiple_of(r * unit, unit), unit)
        gate_ref[rows] = part[:unit].astype(f32)
        up_ref[rows] = part[unit : 2 * unit].astype(f32)
        rows = pl.ds(pl.multiple_of(r * thin, thin), thin)
        for k in range(down_ref.shape[1] // cols):
            at = 2 * unit + k * thin
            down_ref[rows, k * cols : (k + 1) * cols] = part[at : at + thin].astype(f32)


def place_ffn(ring, parts, width):
    wide, units = parts[0].shape
    cols = 256
    return pl.pallas_call(
        functools.partial(place_kernel, ring),
        grid=(units // cols,),
        out_shape=(
            jax.ShapeDtypeStruct((width, units), f32),
            jax.ShapeDtypeStruct((width, units), f32),
            jax.ShapeDtypeStruct((units, width), f32),
        ),
        in_specs=[pl.BlockSpec((wide, cols), lambda j: (0, j))] * len(parts),
        out_specs=(
            pl.BlockSpec((width, cols), lambda j: (0, j)),
            pl.BlockSpec((width, cols), lambda j: (0, j)),
            pl.BlockSpec((cols, width), lambda j: (j, 0)),
        ),
        compiler_params=pltpu.CompilerParams(vmem_limit_bytes=VMEM_BYTES),
        cost_estimate=pl.CostEstimate(
            flops=0, bytes_accessed=18 * width * units, transcendentals=0
        ),
        name="place_ffn",
    )(*parts)


def row_norm(value_rows, gain_vec):
    factor = lax.rsqrt(jnp.mean(value_rows * value_rows, axis=-1, keepdims=True) + EPSILON)
    return (value_rows * factor * gain_vec, factor)


def norm_back(upstream, value_rows, factor, gain_vec):
    inner_grad = upstream * gain_vec
    return factor * (
        inner_grad
        - value_rows * factor * factor * jnp.mean(inner_grad * value_rows, axis=-1, keepdims=True)
    )


def rotate(value_rows, cosine, sines):
    halfway = value_rows.shape[-1] // 2
    leading = value_rows[..., :halfway]
    trailing = value_rows[..., halfway:]
    return jnp.concatenate(
        [leading * cosine - trailing * sines, trailing * cosine + leading * sines], axis=-1
    )


def rotate_back(upstream, cosine, sines):
    return rotate(upstream, cosine, -sines)


def dot(a, b, dims):
    return lax.dot_general(a, b, ((dims[:1], dims[1:]), ((), ())), preferred_element_type=f32)


def on_device(
    tokens,
    cotangent,
    block_order,
    segment_ids,
    norm_gain,
    w_query,
    key_weight,
    value_weight,
    query_gain,
    key_gain,
    w_out,
    ffn_gain,
    w_gate,
    w_up,
    w_down,
):
    devices = lax.axis_size("ctx")
    ring = Ring(devices)
    ring_place, _ = ring.here()
    rows, width = tokens.shape
    seq_count = segment_ids.shape[0]
    blk = rows // seq_count // 2
    tiles = 2 * seq_count
    kv_heads = key_weight.shape[1] // HEAD_SIZE
    query_heads = w_query.shape[1] // HEAD_SIZE
    group = query_heads // kv_heads

    order = block_order[lax.axis_index("ctx")]
    blocks = jnp.stack([order, 2 * devices - 1 - order] * seq_count)
    place = (blocks[:, None] * blk + jnp.arange(blk, dtype=jnp.int32)[None, :]).reshape(rows)
    starts = jnp.stack([jnp.sum((segment_ids < d).astype(jnp.int32), axis=1) for d in (1, 2, 3)], 1)
    inverse = ROPE_BASE ** (-jnp.arange(0, HEAD_SIZE, 2, dtype=f32) / HEAD_SIZE)
    angles = place.astype(f32)[:, None] * inverse[None, :]
    cosine = jnp.cos(angles)[:, None, :]
    sines = jnp.sin(angles)[:, None, :]

    inputs = tokens.astype(f32)
    normed, scale_one = row_norm(inputs, norm_gain)
    hidden_input = normed.astype(bf16)
    query_raw = dot(hidden_input, w_query, (1, 0)).reshape(rows, query_heads, HEAD_SIZE)
    key_raw = dot(hidden_input, key_weight, (1, 0)).reshape(rows, kv_heads, HEAD_SIZE)
    value_rows = dot(hidden_input, value_weight, (1, 0)).astype(bf16)
    query_norm, query_scale = row_norm(query_raw, query_gain)
    key_norm, key_scale = row_norm(key_raw, key_gain)
    queries = rotate(query_norm, cosine, sines).astype(bf16)
    key_rows = rotate(key_norm, cosine, sines).astype(bf16)
    own_kv = jnp.concatenate(
        [key_rows, value_rows.reshape(rows, kv_heads, HEAD_SIZE)], axis=2
    ).reshape(rows, kv_heads * LANES)

    def by_tile(x):
        x = x.reshape(tiles, blk, kv_heads, group, HEAD_SIZE)
        return x.transpose(2, 0, 3, 1, 4).reshape(kv_heads, tiles, group * blk, HEAD_SIZE)

    def by_row(x):
        x = x.reshape(kv_heads, tiles, group, blk, HEAD_SIZE)
        return x.transpose(1, 3, 0, 2, 4).reshape(rows, query_heads, HEAD_SIZE)

    q_tiles = by_tile(queries * jnp.asarray(0.125, bf16))
    q_tiles = jnp.concatenate([q_tiles, jnp.zeros_like(q_tiles)], axis=3)

    attention = Attention(ring, block_order, starts, blk)
    gather = RingGather(ring, own_kv)
    chunks = [own_kv, ring.sibling(own_kv)]
    acc = None
    first = 0
    stages = []
    while True:
        stages.append((first, chunks))
        acc = attention.forward(first, chunks, q_tiles, acc)
        first += len(chunks) // 2
        if first == ring.n:
            break
        chunks = [y for x in gather.step() for y in (x, ring.sibling(x))]
    sums = acc[..., :1]
    attended = acc[..., HEAD_SIZE:] / sums
    attended_low = by_row(attended).reshape(rows, query_heads * HEAD_SIZE).astype(bf16)

    mixed = inputs + sum_over_tp(dot(attended_low, w_out, (1, 0)).astype(bf16))
    normed_two, scale_two = row_norm(mixed, ffn_gain)
    hidden_two = normed_two.astype(bf16)

    gating = dot(hidden_two, w_gate, (1, 0))
    lifted = dot(hidden_two, w_up, (1, 0))
    logistic = jax.nn.sigmoid(gating)
    silu = gating * logistic
    hidden_ffn = (silu * lifted).astype(bf16)
    back_hidden = dot(cotangent, w_down, (1, 1))
    back_gate = (back_hidden * lifted * logistic * (1.0 + gating * (1.0 - logistic))).astype(bf16)
    back_up = (back_hidden * silu).astype(bf16)
    back_part = dot(back_gate, w_gate, (1, 1)) + dot(back_up, w_up, (1, 1))
    back_two = sum_over_tp(back_part.astype(bf16))
    output = (mixed + sum_over_tp(dot(hidden_ffn, w_down, (1, 0)).astype(bf16))).astype(bf16)
    packed = back_gate.shape[1] % 256 == 0 and width % (32 * ring.n) == 0
    if packed:
        keep, give = ffn_grads(ring, hidden_two, back_gate, back_up, hidden_ffn, cotangent)
        got = ring.sibling(give)

        def ffn_terms(d):
            q = (ring_place + d + ring.n) % ring.n
            return [lax.dynamic_index_in_dim(y, q, 0, keepdims=False) for y in (keep, got)]

        ffn_sum = RingSum(ring)
        ffn_sum.far(ffn_terms(ring.n // 2))
    else:
        grad_w_down = dot(hidden_ffn, cotangent, (0, 0)).astype(bf16)
        grad_w_gate = dot(hidden_two, back_gate, (0, 0)).astype(bf16)
        grad_w_up = dot(hidden_two, back_up, (0, 0)).astype(bf16)
        grad_w_gate, grad_w_up, grad_w_down = sum_over_ctx(
            ring, [grad_w_gate, grad_w_up, grad_w_down]
        )

    grad_ffn_gain = jnp.sum(back_two * mixed * scale_two, axis=0)
    back_mixed = cotangent.astype(f32) + norm_back(back_two, mixed, scale_two, ffn_gain)
    back_proj = back_mixed.astype(bf16)
    grad_w_out = dot(attended_low, back_proj, (0, 0)).astype(bf16)
    back_attn = dot(back_proj, w_out, (1, 1)).astype(bf16)

    do_tiles = by_tile(back_attn)
    delta = jnp.sum(do_tiles.astype(f32) * attended, axis=-1)
    do_tiles = jnp.concatenate([jnp.zeros_like(do_tiles), do_tiles], axis=3)
    stats = jnp.stack([jnp.log2(sums[..., 0]), delta], axis=2)
    dq = jnp.zeros((kv_heads, tiles, HEAD_SIZE, group * blk), f32)
    dkv_sum = RingSum(ring)
    waiting = None
    after = []
    d = ring.n // 2
    for first, chunks in reversed(stages):
        if waiting is not None:
            after = []
            if waiting[0] == ring.n // 2:
                dkv_sum.far(waiting[1][0])
            else:
                after += dkv_sum.step(waiting[0], waiting[1][1], waiting[1][0])
        if packed and 0 < d < ring.n // 2:
            after += ffn_sum.step(d, ffn_terms(d), ffn_terms(-d))
        dq, grads = attention.backward(first, chunks, q_tiles, do_tiles, stats, dq, after)
        waiting = d, [(a, ring.sibling(b)) for a, b in zip(grads[::2], grads[1::2])]
        d -= 1
    own_dkv = dkv_sum.sums(waiting[1][0])
    if packed:
        ffn_parts = RingGather(ring, ffn_sum.sums(ffn_terms(0))).all()
        ffn_parts = [y for x in ffn_parts for y in (x, ring.sibling(x))]
        grad_w_gate, grad_w_up, grad_w_down = place_ffn(ring, ffn_parts, width)

    own_dkv = own_dkv.astype(f32).reshape(rows, kv_heads, LANES)

    back_query = by_row(dq.transpose(0, 1, 3, 2)) * 0.125
    turned_query = rotate_back(back_query, cosine, sines)
    grad_query_gain = jnp.sum(turned_query * query_raw * query_scale, axis=(0, 1))
    query_delta = (
        norm_back(turned_query, query_raw, query_scale, query_gain).reshape(rows, -1).astype(bf16)
    )
    turned_key = rotate_back(own_dkv[..., :HEAD_SIZE], cosine, sines)
    grad_key_gain = jnp.sum(turned_key * key_raw * key_scale, axis=(0, 1))
    key_delta = norm_back(turned_key, key_raw, key_scale, key_gain).reshape(rows, -1).astype(bf16)
    value_delta = own_dkv[..., HEAD_SIZE:].reshape(rows, -1).astype(bf16)
    deltas = jnp.concatenate([query_delta, key_delta, value_delta], axis=1)
    weights = jnp.concatenate([w_query, key_weight, value_weight], axis=1)
    back_one = sum_over_tp(dot(deltas, weights, (1, 1)).astype(bf16))
    grad_qkv = dot(hidden_input, deltas, (0, 0)).astype(bf16)
    grad_qkv, grad_w_out = sum_over_ctx(ring, [grad_qkv, grad_w_out])
    q_cols, k_cols = w_query.shape[1], key_weight.shape[1]
    grad_w_query = grad_qkv[:, :q_cols]
    grad_w_key = grad_qkv[:, q_cols : q_cols + k_cols]
    grad_w_value = grad_qkv[:, q_cols + k_cols :]

    grad_norm_gain = jnp.sum(back_one * inputs * scale_one, axis=0)
    input_grad = back_mixed + norm_back(back_one, inputs, scale_one, norm_gain)

    head_gains = sum_over_pairs(
        jnp.concatenate([grad_query_gain, grad_key_gain]), "tp", lax.axis_size("tp")
    )
    gains = sum_over_pairs(
        jnp.concatenate([grad_norm_gain, grad_ffn_gain, head_gains]), "ctx", devices
    )
    return (
        output,
        input_grad,
        gains[:width],
        grad_w_query,
        grad_w_key,
        grad_w_value,
        gains[2 * width : 2 * width + HEAD_SIZE],
        gains[2 * width + HEAD_SIZE :],
        grad_w_out,
        gains[width : 2 * width],
        grad_w_gate,
        grad_w_up,
        grad_w_down,
    )


def solution(mesh):
    return jax.shard_map(
        on_device,
        mesh=mesh,
        in_specs=(
            P("ctx", None),
            P("ctx", None),
            P(),
            P(),
            P(),
            P(None, "tp"),
            P(None, "tp"),
            P(None, "tp"),
            P(),
            P(),
            P("tp", None),
            P(),
            P(None, "tp"),
            P(None, "tp"),
            P("tp", None),
        ),
        out_specs=(
            P("ctx", None),
            P("ctx", None),
            P(),
            P(None, "tp"),
            P(None, "tp"),
            P(None, "tp"),
            P(),
            P(),
            P("tp", None),
            P(),
            P(None, "tp"),
            P(None, "tp"),
            P("tp", None),
        ),
        check_vma=False,
    )
```

time: 1130 us -> 674 us (0.60)
  matrix products: 356 us -> 38.6 us
  waiting for transfers between devices: 447 us -> 243 us
  Pallas kernels: 0 us -> 161 us
  other arithmetic: 198 us -> 79.1 us
  starting transfers between devices: 1.29 us -> 88.8 us
  blocking collectives: 40.6 us -> 0 us
  local copies, waits for them, and re-layouts: 64 us -> 50.4 us
  between operations: 16.2 us -> 3.42 us
    psum x4 -> x0, waiting for transfers between devices: 379 us -> none  [the longest x1 273 us: on_device(): lax.psum(grad_w_query.astype(jnp.bfloat16), 'ctx').astype(jnp.float32)]
    dot_general x27 -> x14, matrix products: 356 us -> 38.6 us  [dot(): lax.dot_general(a, b, ((dims[:1], dims[1:]), ((), ())), preferred_element...]
    ppermute x0 -> x116, waiting for transfers between devices: none -> 243 us  [the longest x32 88 us: left(): return lax.ppermute(x, 'ctx', self.to_left)]
    pallas_call x0 -> x12, Pallas kernels: none -> 161 us  [the longest x5 74.5 us: backward(): pl.pallas_call(functools.partial(backward_kernel, self._make(first, count...]
    convert_element_type x14 -> x25, other arithmetic: 130 us -> 32.3 us  [the longest x23 30.1 us: total(): return out.astype(bf16)]
    ppermute x0 -> x116, starting transfers between devices: none -> 88.8 us  [the longest x32 41.8 us: left(): return lax.ppermute(x, 'ctx', self.to_left)]
    reduce_scatter x2 -> x0, waiting for transfers between devices: 67.1 us -> none  [the longest x1 67.1 us: on_device(): lax.psum_scatter(to_owners(back_value).astype(jnp.bfloat16), 'ctx', scatt...]
    gather x2 -> x0, local copies, waits for them, and re-layouts: 52 us -> none  [the longest x1 48 us: on_device(): all_seg = segment_ids[seq_rows[None, :], all_place]]
  transfers between devices with their start and end apart: 8 -> 116, of which waited for: 5 -> 42; matrix products, arithmetic and copies ran while one was open for 25% -> 18% of each run, Pallas kernels for 0% -> 17%
where the time goes in v1:
time: 674 us; the launch traced here: 665 us
  waiting for transfers between devices  243 us (36%)
  Pallas kernels  161 us (24%)
  starting transfers between devices  88.8 us (13%)
  other arithmetic  79.1 us (12%)
  local copies, waits for them, and re-layouts  50.4 us (7%)
  matrix products  38.6 us (6%)
    ppermute x32, waiting for transfers between devices, left(): return lax.ppermute(x, 'ctx', self.to_left)  88 us
    ppermute x4, waiting for transfers between devices, sum_over_tp(): return x.astype(f32) + lax.ppermute(x, 'tp', [(0, 1), (1, 0)]).astype(f32)  74.6 us
    pallas_call x5, Pallas kernels, backward(): pl.pallas_call(functools.partial(backward_kernel, self._make(first, count...  74.5 us
    ppermute x32, waiting for transfers between devices, right(): return lax.ppermute(x, 'ctx', self.to_right)  60.3 us
    pallas_call x5, Pallas kernels, forward(): pl.pallas_call(functools.partial(forward_kernel, self._make(first, count)...  48.7 us
    ppermute x32, starting transfers between devices, left(): return lax.ppermute(x, 'ctx', self.to_left)  41.8 us
    dot_general x14, matrix products, dot(): lax.dot_general(a, b, ((dims[:1], dims[1:]), ((), ())), preferred_element...  38.6 us
    ppermute x32, starting transfers between devices, right(): return lax.ppermute(x, 'ctx', self.to_right)  31.7 us
  transfers between devices with their start and end apart: 116, of which 42 were waited for; matrix products, arithmetic and copies ran while one was open for 18% of the time, Pallas kernels for 17%

profile of v1, /device:TPU:0, one launch (start us, length us, event | category | flops | bytes accessed | tf_op | source)
XLA Modules:
  0.0 665.0 jit_solution(4631452515209179552)
XLA Ops:
  20.0 12.0 %collective-permute-done.4.refs_2_ = bf16[512,512]{1,0:T(8,128)(2,1)} collective-permute-done((bf16[512,512]{1,0:T(8,128)(2,1)}, bf16[512,512]{1,0:T(8,128)(2,1)}, u32[]{:S(2)}, u32[]{:S(2)}) %collective-permute-start.4) | collective-permute-done | bytes 524320 | tf_op jit(solution)/shard_map/ppermute | solution.py:65
  36.8 9.2 %collective-permute-done.5.refs_2_ = bf16[512,512]{1,0:T(8,128)(2,1)} collective-permute-done((bf16[512,512]{1,0:T(8,128)(2,1)}, bf16[512,512]{1,0:T(8,128)(2,1)}, u32[]{:S(2)}, u32[]{:S(2)}) %collective-permute-start.5) | collective-permute-done | bytes 524320 | tf_op jit(solution)/shard_map/ppermute | solution.py:65
  54.0 7.6 %attend_forward.5.refs_4_ = f32[4,2,512,128]{3,2,1,0:T(8,128)} custom-call(s32[16]{0:T(128)} %order_ref.19, s32[1,3]{1,0:T(1,128)} %pad_add_fusion.starts_ref, bf16[4,2,512,128]{3,2,1,0:T(8,128)(2,1)} %concatenate.86.q_ref, bf16[512,512]{1,0:T(8,128)(2,1)} %bitcast.160.refs_0_, bf16[512,512]{1,0:T(8,128)(2,1)} %collective-permute-done.15.refs_1_), custom_call_target="tpu_custom_call" | custom-call | flops 2684354560 | bytes 6291456 | tf_op jit(solution)/shard_map/attend_forward/pallas_call | solution.py:345
  66.6 11.3 %attend_forward.6.refs_4_ = f32[4,2,512,128]{3,2,1,0:T(8,128)} custom-call(s32[16]{0:T(128)} %order_ref.19, s32[1,3]{1,0:T(1,128)} %pad_add_fusion.starts_ref, bf16[4,2,512,128]{3,2,1,0:T(8,128)(2,1)} %concatenate.86.q_ref, bf16[512,512]{1,0:T(8,128)(2,1)} %collective-permute-done.refs_0_, bf16[512,512]{1,0:T(8,128)(2,1)} %collective-permute-done.13.refs_1_, ...), custom_call_target="tpu_custom_call" | custom-call | flops 4294967296 | bytes 7340032 | tf_op jit(solution)/shard_map/attend_forward/pallas_call | solution.py:345
  80.3 11.3 %attend_forward.7.refs_4_ = f32[4,2,512,128]{3,2,1,0:T(8,128)} custom-call(s32[16]{0:T(128)} %order_ref.19, s32[1,3]{1,0:T(1,128)} %pad_add_fusion.starts_ref, bf16[4,2,512,128]{3,2,1,0:T(8,128)(2,1)} %concatenate.86.q_ref, bf16[512,512]{1,0:T(8,128)(2,1)} %collective-permute-done.1.refs_0_, bf16[512,512]{1,0:T(8,128)(2,1)} %copy-done.74, ...), custom_call_target="tpu_custom_call" | custom-call | flops 4294967296 | bytes 7340032 | tf_op jit(solution)/shard_map/attend_forward/pallas_call | solution.py:345
  93.2 11.3 %attend_forward.8.refs_2_ = f32[4,2,512,128]{3,2,1,0:T(8,128)} custom-call(s32[16]{0:T(128)} %order_ref.19, s32[1,3]{1,0:T(1,128)} %pad_add_fusion.starts_ref, bf16[4,2,512,128]{3,2,1,0:T(8,128)(2,1)} %concatenate.86.q_ref, bf16[512,512]{1,0:T(8,128)(2,1)} %collective-permute-done.2.refs_0_, bf16[512,512]{1,0:T(8,128)(2,1)} %copy-done.76, ...), custom_call_target="tpu_custom_call" | custom-call | flops 4294967296 | bytes 7340032 | tf_op jit(solution)/shard_map/attend_forward/pallas_call | solution.py:345
  105.2 7.3 %attend_forward.9 = f32[4,2,512,128]{3,2,1,0:T(8,128)} custom-call(s32[16]{0:T(128)} %order_ref.19, s32[1,3]{1,0:T(1,128)} %pad_add_fusion.starts_ref, bf16[4,2,512,128]{3,2,1,0:T(8,128)(2,1)} %concatenate.86.q_ref, bf16[512,512]{1,0:T(8,128)(2,1)} %copy-done.51, bf16[512,512]{1,0:T(8,128)(2,1)} %copy-done.77, f32[4,2,512,128]{3,2,1,0:T(8,128)} %attend_forward.8.refs_2_), custom_call_target="tpu_custom_call" | custom-call | flops 2147483648 | bytes 6291456 | tf_op jit(solution)/shard_map/attend_forward/pallas_call | solution.py:345
  125.1 5.1 fusion.64
  130.2 18.8 %collective-permute-done.16 = bf16[512,1024]{1,0:T(8,128)(2,1)S(1)} collective-permute-done((bf16[512,1024]{1,0:T(8,128)(2,1)S(1)}, bf16[512,1024]{1,0:T(8,128)(2,1)S(1)}, u32[]{:S(2)}, u32[]{:S(2)}) %collective-permute-start.16) | collective-permute-done | bytes 1048608 | tf_op jit(solution)/shard_map/ppermute | solution.py:185
  153.0 6.2 multiply_convert_fusion
  159.2 4.0 fusion.65
  163.2 21.8 %ffn_grads.1 = (bf16[8,192,2304]{2,1,0:T(8,128)(2,1)}, bf16[8,192,2304]{2,1,0:T(8,128)(2,1)}) custom-call(bf16[512,1024]{1,0:T(8,128)(2,1)} %copy-done.27, bf16[512,2304]{1,0:T(8,128)(2,1)} %copy-done.78, bf16[512,2304]{1,0:T(8,128)(2,1)} %get-tuple-element.88.up_ref, bf16[512,2304]{1,0:T(8,128)(2,1)} %get-tuple-element.90.ffn_ref, bf16[512,1024]{1,0:T(8,128)(2,1)} %cot_ref.1), custom_call_target="tpu_custom_call" | custom-call | flops 7247757312 | bytes 20971520 | tf_op jit(solution)/shard_map/ffn_grads/pallas_call | solution.py:424
  185.1 6.0 add_convert_fusion
  196.8 20.7 %collective-permute-done.18 = bf16[512,1024]{1,0:T(8,128)(2,1)} collective-permute-done((bf16[512,1024]{1,0:T(8,128)(2,1)}, bf16[512,1024]{1,0:T(8,128)(2,1)}, u32[]{:S(2)}, u32[]{:S(2)}) %collective-permute-start.18) | collective-permute-done | bytes 1048608 | tf_op jit(solution)/shard_map/ppermute | solution.py:185
  220.4 19.4 %collective-permute-done.17 = bf16[512,1024]{1,0:T(8,128)(2,1)} collective-permute-done((bf16[512,1024]{1,0:T(8,128)(2,1)}, bf16[512,1024]{1,0:T(8,128)(2,1)}, u32[]{:S(2)}, u32[]{:S(2)}) %collective-permute-start.17) | collective-permute-done | bytes 1048608 | tf_op jit(solution)/shard_map/ppermute | solution.py:185
  239.8 4.9 multiply_add_fusion
  276.1 10.1 %attend_backward.5 = (f32[4,2,64,512]{3,2,1,0:T(8,128)}, f32[512,512]{1,0:T(8,128)}, bf16[512,512]{1,0:T(8,128)(2,1)}) custom-call(s32[16]{0:T(128)} %order_ref.19, s32[1,3]{1,0:T(1,128)} %pad_add_fusion.starts_ref, bf16[4,2,512,128]{3,2,1,0:T(8,128)(2,1)} %concatenate.86.q_ref, bf16[4,2,512,128]{3,2,1,0:T(8,128)(2,1)} %concatenate.89.do_ref, ...), custom_call_target="tpu_custom_call" | custom-call | flops 5368709120 | bytes 6815744 | tf_op jit(solution)/shard_map/attend_backward/pallas_call | solution.py:363
  301.7 6.0 collective-permute-done.87
  314.1 10.1 %collective-permute-done.20 = bf16[96,2304]{1,0:T(8,128)(2,1)S(1)} collective-permute-done((bf16[96,2304]{1,0:T(8,128)(2,1)S(1)}, bf16[96,2304]{1,0:T(8,128)(2,1)S(1)}, u32[]{:S(2)}, u32[]{:S(2)}) %collective-permute-start.20) | collective-permute-done | bytes 442400 | tf_op jit(solution)/shard_map/ppermute | solution.py:62
  328.2 17.5 %attend_backward.6 = (f32[4,2,64,512]{3,2,1,0:T(8,128)}, f32[512,512]{1,0:T(8,128)}, bf16[512,512]{1,0:T(8,128)(2,1)}, f32[512,512]{1,0:T(8,128)}, bf16[512,512]{1,0:T(8,128)(2,1)}) custom-call(s32[16]{0:T(128)} %order_ref.19, s32[1,3]{1,0:T(1,128)} %pad_add_fusion.starts_ref, bf16[4,2,512,128]{3,2,1,0:T(8,128)(2,1)} %concatenate.86.q_ref, ...), custom_call_target="tpu_custom_call" | custom-call | flops 10737418240 | bytes 9437184 | tf_op jit(solution)/shard_map/attend_backward/pallas_call | solution.py:363
  352.6 22.5 %collective-permute-done.26 = bf16[256,512]{1,0:T(8,128)(2,1)S(1)} collective-permute-done((bf16[256,512]{1,0:T(8,128)(2,1)S(1)}, bf16[256,512]{1,0:T(8,128)(2,1)S(1)}, u32[]{:S(2)}, u32[]{:S(2)}) %collective-permute-start.26) | collective-permute-done | bytes 262176 | tf_op jit(solution)/shard_map/ppermute | solution.py:65
  382.1 17.5 %attend_backward.7 = (f32[4,2,64,512]{3,2,1,0:T(8,128)}, f32[512,512]{1,0:T(8,128)}, bf16[512,512]{1,0:T(8,128)(2,1)}, f32[512,512]{1,0:T(8,128)}, bf16[512,512]{1,0:T(8,128)(2,1)}) custom-call(s32[16]{0:T(128)} %order_ref.19, s32[1,3]{1,0:T(1,128)} %pad_add_fusion.starts_ref, bf16[4,2,512,128]{3,2,1,0:T(8,128)(2,1)} %concatenate.86.q_ref, ...), custom_call_target="tpu_custom_call" | custom-call | flops 10737418240 | bytes 9437184 | tf_op jit(solution)/shard_map/attend_backward/pallas_call | solution.py:363
  406.8 8.9 %collective-permute-done.32 = bf16[512,512]{1,0:T(8,128)(2,1)S(1)} collective-permute-done((bf16[512,512]{1,0:T(8,128)(2,1)}, bf16[512,512]{1,0:T(8,128)(2,1)S(1)}, u32[]{:S(2)}, u32[]{:S(2)}) %collective-permute-start.32) | collective-permute-done | bytes 524320 | tf_op jit(solution)/shard_map/ppermute | solution.py:65
  417.5 16.4 %collective-permute-done.34 = bf16[192,2304]{1,0:T(8,128)(2,1)S(1)} collective-permute-done((bf16[192,2304]{1,0:T(8,128)(2,1)S(1)}, bf16[192,2304]{1,0:T(8,128)(2,1)S(1)}, u32[]{:S(2)}, u32[]{:S(2)}) %collective-permute-start.34) | collective-permute-done | bytes 884768 | tf_op jit(solution)/shard_map/ppermute | solution.py:65
  437.7 17.5 %attend_backward.8 = (f32[4,2,64,512]{3,2,1,0:T(8,128)}, f32[512,512]{1,0:T(8,128)}, bf16[512,512]{1,0:T(8,128)(2,1)}, f32[512,512]{1,0:T(8,128)}, bf16[512,512]{1,0:T(8,128)(2,1)}) custom-call(s32[16]{0:T(128)} %order_ref.19, s32[1,3]{1,0:T(1,128)} %pad_add_fusion.starts_ref, bf16[4,2,512,128]{3,2,1,0:T(8,128)(2,1)} %concatenate.86.q_ref, ...), custom_call_target="tpu_custom_call" | custom-call | flops 10737418240 | bytes 9437184 | tf_op jit(solution)/shard_map/attend_backward/pallas_call | solution.py:363
  461.4 8.6 %collective-permute-done.38 = bf16[512,512]{1,0:T(8,128)(2,1)S(1)} collective-permute-done((bf16[512,512]{1,0:T(8,128)(2,1)S(1)}, bf16[512,512]{1,0:T(8,128)(2,1)S(1)}, u32[]{:S(2)}, u32[]{:S(2)}) %collective-permute-start.38) | collective-permute-done | bytes 524320 | tf_op jit(solution)/shard_map/ppermute | solution.py:65
  472.7 11.9 %attend_backward.9 = (f32[4,2,64,512]{3,2,1,0:T(8,128)}, f32[512,512]{1,0:T(8,128)}, bf16[512,512]{1,0:T(8,128)(2,1)}) custom-call(s32[16]{0:T(128)} %order_ref.19, s32[1,3]{1,0:T(1,128)} %pad_add_fusion.starts_ref, bf16[4,2,512,128]{3,2,1,0:T(8,128)(2,1)} %concatenate.86.q_ref, bf16[4,2,512,128]{3,2,1,0:T(8,128)(2,1)} %concatenate.89.do_ref, ...), custom_call_target="tpu_custom_call" | custom-call | flops 6710886400 | bytes 6815744 | tf_op jit(solution)/shard_map/attend_backward/pallas_call | solution.py:363
  524.8 15.6 %collective-permute-done.42 = bf16[512,1024]{1,0:T(8,128)(2,1)S(1)} collective-permute-done((bf16[512,1024]{1,0:T(8,128)(2,1)S(1)}, bf16[512,1024]{1,0:T(8,128)(2,1)S(1)}, u32[]{:S(2)}, u32[]{:S(2)}) %collective-permute-start.42) | collective-permute-done | bytes 1048608 | tf_op jit(solution)/shard_map/ppermute | solution.py:185
  555.9 16.8 %collective-permute-done.46 = f32[2176]{0:T(1024)S(1)} collective-permute-done((f32[2176]{0:T(1024)S(1)}, f32[2176]{0:T(1024)S(1)}, u32[]{:S(2)}, u32[]{:S(2)}) %collective-permute-start.46) | collective-permute-done | bytes 8736 | tf_op jit(solution)/shard_map/ppermute | solution.py:177
  607.5 18.1 %collective-permute-done.70 = bf16[32,1024]{1,0:T(8,128)(2,1)S(1)} collective-permute-done((bf16[32,1024]{1,0:T(8,128)(2,1)S(1)}, bf16[32,1024]{1,0:T(8,128)(2,1)S(1)}, u32[]{:S(2)}, u32[]{:S(2)}) %collective-permute-start.70) | collective-permute-done | bytes 65568 | tf_op jit(solution)/shard_map/ppermute | solution.py:62
  629.1 10.0 %collective-permute-done.113 = bf16[96,2304]{1,0:T(8,128)(2,1)S(1)} collective-permute-done((bf16[96,2304]{1,0:T(8,128)(2,1)S(1)}, bf16[96,2304]{1,0:T(8,128)(2,1)S(1)}, u32[]{:S(2)}, u32[]{:S(2)}) %collective-permute-start.113) | collective-permute-done | bytes 442400 | tf_op jit(solution)/shard_map/ppermute | solution.py:62
  648.4 16.2 %place_ffn.1 = (f32[1024,2304]{1,0:T(8,128)}, f32[1024,2304]{1,0:T(8,128)}, f32[2304,1024]{1,0:T(8,128)}) custom-call(bf16[192,2304]{1,0:T(8,128)(2,1)} %copy-done.12, bf16[192,2304]{1,0:T(8,128)(2,1)} %copy-done.32, bf16[192,2304]{1,0:T(8,128)(2,1)} %copy-done.29, bf16[192,2304]{1,0:T(8,128)(2,1)} %copy-done.34, bf16[192,2304]{1,0:T(8,128)(2,1)} %copy-done.28, ...), custom_call_target="tpu_custom_call" | custom-call | bytes 42467328 | tf_op jit(solution)/shard_map/place_ffn/pallas_call | solution.py:462
  (577 shorter events, 261.2 us)
Async XLA Ops:
  16.0 37.9 %collective-permute-start.15 = (bf16[512,512]{1,0:T(8,128)(2,1)}, bf16[512,512]{1,0:T(8,128)(2,1)}, u32[]{:S(2)}, u32[]{:S(2)}) collective-permute-start(bf16[512,512]{1,0:T(8,128)(2,1)} %bitcast.160.refs_0_), channel_id=1, source_target_pairs={{0,2},{2,0},{4,6},{6,4},{8,10},{10,8},{12,14},{14,12},{16,18},{18,... | collective-permute-start | bytes 1572872 | tf_op jit(solution)/shard_map/ppermute | solution.py:68
  36.3 29.3 %collective-permute-start.14 = (bf16[512,512]{1,0:T(8,128)(2,1)}, bf16[512,512]{1,0:T(8,128)(2,1)}, u32[]{:S(2)}, u32[]{:S(2)}) collective-permute-start(bf16[512,512]{1,0:T(8,128)(2,1)} %collective-permute-done.4.refs_2_), channel_id=1, source_target_pairs={{0,2},{2,0},{4,6},{6,4},{8,10},{10,8},{12,14},{14,12},{16,18},{18,... | collective-permute-start | bytes 1572872 | tf_op jit(solution)/shard_map/ppermute | solution.py:68
  36.3 30.3 %collective-permute-start.13 = (bf16[512,512]{1,0:T(8,128)(2,1)}, bf16[512,512]{1,0:T(8,128)(2,1)}, u32[]{:S(2)}, u32[]{:S(2)}) collective-permute-start(bf16[512,512]{1,0:T(8,128)(2,1)} %collective-permute-done.refs_0_), channel_id=1, source_target_pairs={{0,2},{2,0},{4,6},{6,4},{8,10},{10,8},{12,14},{14,12},{16,18},{18,... | collective-permute-start | bytes 1572872 | tf_op jit(solution)/shard_map/ppermute | solution.py:68
  78.5 26.0 %collective-permute-start.8 = (bf16[512,512]{1,0:T(8,128)(2,1)S(1)}, bf16[512,512]{1,0:T(8,128)(2,1)S(1)}, u32[]{:S(2)}, u32[]{:S(2)}) collective-permute-start(bf16[512,512]{1,0:T(8,128)(2,1)S(1)} %constant_dynamic-update-slice_fusion.refs_0_), channel_id=1, source_target_pairs={{0,2},{2,0},{4,6},{6,4},{8,10},{10,8},{12,14},{14,12},{16,18},{18,... | collective-permute-start | bytes 1572872 | tf_op jit(solution)/shard_map/ppermute | solution.py:68
  185.0 124.5 %collective-permute-start.19 = (bf16[8,192,2304]{2,1,0:T(8,128)(2,1)}, bf16[8,192,2304]{2,1,0:T(8,128)(2,1)}, u32[]{:S(2)}, u32[]{:S(2)}) collective-permute-start(bf16[8,192,2304]{2,1,0:T(8,128)(2,1)} %get-tuple-element.41), channel_id=1, source_target_pairs={{0,2},{2,0},{4,6},{6,4},{8,10},{10,8},{12,14},{14,12},{16,18},{18,... | collective-permute-start | bytes 21233672 | tf_op jit(solution)/shard_map/ppermute | solution.py:68
  191.1 26.4 %collective-permute-start.18 = (bf16[512,1024]{1,0:T(8,128)(2,1)}, bf16[512,1024]{1,0:T(8,128)(2,1)}, u32[]{:S(2)}, u32[]{:S(2)}) collective-permute-start(bf16[512,1024]{1,0:T(8,128)(2,1)} %add_convert_fusion), channel_id=1, source_target_pairs={{0,1},{1,0},{2,3},{3,2},{4,5},{5,4},{6,7},{7,6},{8,9},{9,8},{10,11... | collective-permute-start | bytes 3145736 | tf_op jit(solution)/shard_map/ppermute | solution.py:185
  196.2 43.6 %collective-permute-start.17 = (bf16[512,1024]{1,0:T(8,128)(2,1)}, bf16[512,1024]{1,0:T(8,128)(2,1)}, u32[]{:S(2)}, u32[]{:S(2)}) collective-permute-start(bf16[512,1024]{1,0:T(8,128)(2,1)} %convolution_convert_fusion.1), channel_id=1, source_target_pairs={{0,1},{1,0},{2,3},{3,2},{4,5},{5,4},{6,7},{7,6},{8,9},{9,8},{10,11... | collective-permute-start | bytes 3145736 | tf_op jit(solution)/shard_map/ppermute | solution.py:185
  297.7 51.4 %collective-permute-start.24 = (bf16[256,512]{1,0:T(8,128)(2,1)S(1)}, bf16[256,512]{1,0:T(8,128)(2,1)S(1)}, u32[]{:S(2)}, u32[]{:S(2)}) collective-permute-start(bf16[256,512]{1,0:T(8,128)(2,1)S(1)} %get-tuple-element.117), channel_id=1, source_target_pairs={{0,8},{2,10},{8,16},{10,18},{16,24},{18,26},{24,28},{26,30},{28,20... | collective-permute-start | bytes 786440 | tf_op jit(solution)/shard_map/ppermute | solution.py:62
  307.7 38.6 %collective-permute-start.91 = (bf16[32,1024]{1,0:T(8,128)(2,1)S(1)}, bf16[32,1024]{1,0:T(8,128)(2,1)S(1)}, u32[]{:S(2)}, u32[]{:S(2)}) collective-permute-start(bf16[32,1024]{1,0:T(8,128)(2,1)S(1)} %collective-permute-done.87), channel_id=1, source_target_pairs={{0,8},{2,10},{8,16},{10,18},{16,24},{18,26},{24,28},{26,30},{28,20... | collective-permute-start | bytes 196616 | tf_op jit(solution)/shard_map/ppermute | solution.py:62
  314.0 31.7 %collective-permute-start.88 = (bf16[32,1024]{1,0:T(8,128)(2,1)S(1)}, bf16[32,1024]{1,0:T(8,128)(2,1)S(1)}, u32[]{:S(2)}, u32[]{:S(2)}) collective-permute-start(bf16[32,1024]{1,0:T(8,128)(2,1)S(1)} %collective-permute-done.87), channel_id=1, source_target_pairs={{0,2},{2,0},{4,6},{6,4},{8,10},{10,8},{12,14},{14,12},{16,18},{18,... | collective-permute-start | bytes 196616 | tf_op jit(solution)/shard_map/ppermute | solution.py:68
  346.3 30.2 %collective-permute-start.25 = (bf16[512,512]{1,0:T(8,128)(2,1)}, bf16[512,512]{1,0:T(8,128)(2,1)S(1)}, u32[]{:S(2)}, u32[]{:S(2)}) collective-permute-start(bf16[512,512]{1,0:T(8,128)(2,1)} %get-tuple-element.48), channel_id=1, source_target_pairs={{0,2},{2,0},{4,6},{6,4},{8,10},{10,8},{12,14},{14,12},{16,18},{18,... | collective-permute-start | bytes 1572872 | tf_op jit(solution)/shard_map/ppermute | solution.py:68
  347.0 30.5 %collective-permute-start.27 = (bf16[192,2304]{1,0:T(8,128)(2,1)S(1)}, bf16[192,2304]{1,0:T(8,128)(2,1)S(1)}, u32[]{:S(2)}, u32[]{:S(2)}) collective-permute-start(bf16[192,2304]{1,0:T(8,128)(2,1)S(1)} %copy-done.40), channel_id=1, source_target_pairs={{0,8},{2,10},{8,16},{10,18},{16,24},{18,26},{24,28},{26,30},{28,20... | collective-permute-start | bytes 2654216 | tf_op jit(solution)/shard_map/ppermute | solution.py:62
  347.1 31.2 %collective-permute-start.28 = (bf16[192,2304]{1,0:T(8,128)(2,1)S(1)}, bf16[192,2304]{1,0:T(8,128)(2,1)S(1)}, u32[]{:S(2)}, u32[]{:S(2)}) collective-permute-start(bf16[192,2304]{1,0:T(8,128)(2,1)S(1)} %copy-done.39), channel_id=1, source_target_pairs={{8,0},{10,2},{16,8},{18,10},{24,16},{26,18},{28,24},{30,26},{20,28... | collective-permute-start | bytes 2654216 | tf_op jit(solution)/shard_map/ppermute | solution.py:65
  349.1 25.9 %collective-permute-start.26 = (bf16[256,512]{1,0:T(8,128)(2,1)S(1)}, bf16[256,512]{1,0:T(8,128)(2,1)S(1)}, u32[]{:S(2)}, u32[]{:S(2)}) collective-permute-start(bf16[256,512]{1,0:T(8,128)(2,1)S(1)} %get-tuple-element.118), channel_id=1, source_target_pairs={{8,0},{10,2},{16,8},{18,10},{24,16},{26,18},{28,24},{30,26},{20,28... | collective-permute-start | bytes 786440 | tf_op jit(solution)/shard_map/ppermute | solution.py:65
  350.6 49.2 %collective-permute-start.95 = (bf16[16,1024]{1,0:T(8,128)(2,1)S(1)}, bf16[16,1024]{1,0:T(8,128)(2,1)}, u32[]{:S(2)}, u32[]{:S(2)}) collective-permute-start(bf16[16,1024]{1,0:T(8,128)(2,1)S(1)} %slice.339), channel_id=1, source_target_pairs={{0,8},{2,10},{8,16},{10,18},{16,24},{18,26},{24,28},{26,30},{28,20... | collective-permute-start | bytes 98312 | tf_op jit(solution)/shard_map/ppermute | solution.py:62
  375.0 26.9 %collective-permute-start.96 = (bf16[16,1024]{1,0:T(8,128)(2,1)}, bf16[16,1024]{1,0:T(8,128)(2,1)}, u32[]{:S(2)}, u32[]{:S(2)}) collective-permute-start(bf16[16,1024]{1,0:T(8,128)(2,1)} %slice.340), channel_id=1, source_target_pairs={{8,0},{10,2},{16,8},{18,10},{24,16},{26,18},{28,24},{30,26},{20,28... | collective-permute-start | bytes 98312 | tf_op jit(solution)/shard_map/ppermute | solution.py:65
  376.5 26.7 %collective-permute-start.92 = (bf16[32,1024]{1,0:T(8,128)(2,1)S(1)}, bf16[32,1024]{1,0:T(8,128)(2,1)S(1)}, u32[]{:S(2)}, u32[]{:S(2)}) collective-permute-start(bf16[32,1024]{1,0:T(8,128)(2,1)S(1)} %collective-permute-done.91), channel_id=1, source_target_pairs={{0,2},{2,0},{4,6},{6,4},{8,10},{10,8},{12,14},{14,12},{16,18},{18,... | collective-permute-start | bytes 196616 | tf_op jit(solution)/shard_map/ppermute | solution.py:68
  377.5 26.4 %collective-permute-start.30 = (bf16[512,512]{1,0:T(8,128)(2,1)S(1)}, bf16[512,512]{1,0:T(8,128)(2,1)S(1)}, u32[]{:S(2)}, u32[]{:S(2)}) collective-permute-start(bf16[512,512]{1,0:T(8,128)(2,1)S(1)} %get-tuple-element.146.refs_4_), channel_id=1, source_target_pairs={{0,8},{2,10},{8,16},{10,18},{16,24},{18,26},{24,28},{26,30},{28,20... | collective-permute-start | bytes 1572872 | tf_op jit(solution)/shard_map/ppermute | solution.py:62
  401.9 32.0 %collective-permute-start.34 = (bf16[192,2304]{1,0:T(8,128)(2,1)S(1)}, bf16[192,2304]{1,0:T(8,128)(2,1)S(1)}, u32[]{:S(2)}, u32[]{:S(2)}) collective-permute-start(bf16[192,2304]{1,0:T(8,128)(2,1)S(1)} %copy-done.42), channel_id=1, source_target_pairs={{8,0},{10,2},{16,8},{18,10},{24,16},{26,18},{28,24},{30,26},{20,28... | collective-permute-start | bytes 2654216 | tf_op jit(solution)/shard_map/ppermute | solution.py:65
  403.2 30.7 %collective-permute-start.33 = (bf16[192,2304]{1,0:T(8,128)(2,1)S(1)}, bf16[192,2304]{1,0:T(8,128)(2,1)S(1)}, u32[]{:S(2)}, u32[]{:S(2)}) collective-permute-start(bf16[192,2304]{1,0:T(8,128)(2,1)S(1)} %copy-done.41), channel_id=1, source_target_pairs={{0,8},{2,10},{8,16},{10,18},{16,24},{18,26},{24,28},{26,30},{28,20... | collective-permute-start | bytes 2654216 | tf_op jit(solution)/shard_map/ppermute | solution.py:62
  404.8 52.0 %collective-permute-start.94 = (bf16[32,1024]{1,0:T(8,128)(2,1)S(1)}, bf16[32,1024]{1,0:T(8,128)(2,1)S(1)}, u32[]{:S(2)}, u32[]{:S(2)}) collective-permute-start(bf16[32,1024]{1,0:T(8,128)(2,1)S(1)} %collective-permute-done.93), channel_id=1, source_target_pairs={{0,2},{2,0},{4,6},{6,4},{8,10},{10,8},{12,14},{14,12},{16,18},{18,... | collective-permute-start | bytes 196616 | tf_op jit(solution)/shard_map/ppermute | solution.py:68
  415.6 134.0 %collective-permute-start.97 = (bf16[32,1024]{1,0:T(8,128)(2,1)S(1)}, bf16[32,1024]{1,0:T(8,128)(2,1)S(1)}, u32[]{:S(2)}, u32[]{:S(2)}) collective-permute-start(bf16[32,1024]{1,0:T(8,128)(2,1)S(1)} %constant_dynamic-update-slice_fusion.4), channel_id=1, source_target_pairs={{0,2},{2,0},{4,6},{6,4},{8,10},{10,8},{12,14},{14,12},{16,18},{18,... | collective-permute-start | bytes 196616 | tf_op jit(solution)/shard_map/ppermute | solution.py:68
  415.6 41.4 %collective-permute-start.36 = (bf16[512,512]{1,0:T(8,128)(2,1)S(1)}, bf16[512,512]{1,0:T(8,128)(2,1)S(1)}, u32[]{:S(2)}, u32[]{:S(2)}) collective-permute-start(bf16[512,512]{1,0:T(8,128)(2,1)S(1)} %add_convert_fusion.6.refs_4_), channel_id=1, source_target_pairs={{0,8},{2,10},{8,16},{10,18},{16,24},{18,26},{24,28},{26,30},{28,20... | collective-permute-start | bytes 1572872 | tf_op jit(solution)/shard_map/ppermute | solution.py:62
  457.0 61.0 %collective-permute-start.99 = (bf16[192,2304]{1,0:T(8,128)(2,1)}, bf16[192,2304]{1,0:T(8,128)(2,1)}, u32[]{:S(2)}, u32[]{:S(2)}) collective-permute-start(bf16[192,2304]{1,0:T(8,128)(2,1)} %get-tuple-element.78.refs_7_), channel_id=1, source_target_pairs={{8,0},{10,2},{16,8},{18,10},{24,16},{26,18},{28,24},{30,26},{20,28... | collective-permute-start | bytes 2654216 | tf_op jit(solution)/shard_map/ppermute | solution.py:65
  460.4 37.2 %collective-permute-start.40 = (bf16[512,512]{1,0:T(8,128)(2,1)}, bf16[512,512]{1,0:T(8,128)(2,1)}, u32[]{:S(2)}, u32[]{:S(2)}) collective-permute-start(bf16[512,512]{1,0:T(8,128)(2,1)} %add_convert_fusion.4.refs_2_), channel_id=1, source_target_pairs={{0,8},{2,10},{8,16},{10,18},{16,24},{18,26},{24,28},{26,30},{28,20... | collective-permute-start | bytes 1572872 | tf_op jit(solution)/shard_map/ppermute | solution.py:62
  471.0 28.9 %collective-permute-start.41 = (bf16[512,512]{1,0:T(8,128)(2,1)}, bf16[512,512]{1,0:T(8,128)(2,1)}, u32[]{:S(2)}, u32[]{:S(2)}) collective-permute-start(bf16[512,512]{1,0:T(8,128)(2,1)} %add_convert_fusion.3.refs_3_), channel_id=1, source_target_pairs={{8,0},{10,2},{16,8},{18,10},{24,16},{26,18},{28,24},{30,26},{20,28... | collective-permute-start | bytes 1572872 | tf_op jit(solution)/shard_map/ppermute | solution.py:65
  522.6 27.6 %collective-permute-start.103 = (bf16[192,2304]{1,0:T(8,128)(2,1)S(1)}, bf16[192,2304]{1,0:T(8,128)(2,1)S(1)}, u32[]{:S(2)}, u32[]{:S(2)}) collective-permute-start(bf16[192,2304]{1,0:T(8,128)(2,1)S(1)} %fusion.21.refs_0_), channel_id=1, source_target_pairs={{8,0},{10,2},{16,8},{18,10},{24,16},{26,18},{28,24},{30,26},{20,28... | collective-permute-start | bytes 2654216 | tf_op jit(solution)/shard_map/ppermute | solution.py:65
  523.7 27.0 %collective-permute-start.101 = (bf16[192,2304]{1,0:T(8,128)(2,1)S(1)}, bf16[192,2304]{1,0:T(8,128)(2,1)S(1)}, u32[]{:S(2)}, u32[]{:S(2)}) collective-permute-start(bf16[192,2304]{1,0:T(8,128)(2,1)S(1)} %fusion.21.refs_0_), channel_id=1, source_target_pairs={{0,8},{2,10},{8,16},{10,18},{16,24},{18,26},{24,28},{26,30},{28,20... | collective-permute-start | bytes 2654216 | tf_op jit(solution)/shard_map/ppermute | solution.py:62
  550.3 49.6 %collective-permute-start.107 = (bf16[192,2304]{1,0:T(8,128)(2,1)S(1)}, bf16[192,2304]{1,0:T(8,128)(2,1)S(1)}, u32[]{:S(2)}, u32[]{:S(2)}) collective-permute-start(bf16[192,2304]{1,0:T(8,128)(2,1)S(1)} %collective-permute-done.103.refs_4_), channel_id=1, source_target_pairs={{8,0},{10,2},{16,8},{18,10},{24,16},{26,18},{28,24},{30,26},{20,28... | collective-permute-start | bytes 2654216 | tf_op jit(solution)/shard_map/ppermute | solution.py:65
  550.8 49.2 %collective-permute-start.105 = (bf16[192,2304]{1,0:T(8,128)(2,1)S(1)}, bf16[192,2304]{1,0:T(8,128)(2,1)S(1)}, u32[]{:S(2)}, u32[]{:S(2)}) collective-permute-start(bf16[192,2304]{1,0:T(8,128)(2,1)S(1)} %collective-permute-done.101.refs_2_), channel_id=1, source_target_pairs={{0,8},{2,10},{8,16},{10,18},{16,24},{18,26},{24,28},{26,30},{28,20... | collective-permute-start | bytes 2654216 | tf_op jit(solution)/shard_map/ppermute | solution.py:62
  599.9 39.9 %collective-permute-start.100 = (bf16[192,2304]{1,0:T(8,128)(2,1)S(1)}, bf16[192,2304]{1,0:T(8,128)(2,1)S(1)}, u32[]{:S(2)}, u32[]{:S(2)}) collective-permute-start(bf16[192,2304]{1,0:T(8,128)(2,1)S(1)} %fusion.21.refs_0_), channel_id=1, source_target_pairs={{0,2},{2,0},{4,6},{6,4},{8,10},{10,8},{12,14},{14,12},{16,18},{18,... | collective-permute-start | bytes 2654216 | tf_op jit(solution)/shard_map/ppermute | solution.py:68
  600.0 27.6 %collective-permute-start.111 = (bf16[192,2304]{1,0:T(8,128)(2,1)S(1)}, bf16[192,2304]{1,0:T(8,128)(2,1)S(1)}, u32[]{:S(2)}, u32[]{:S(2)}) collective-permute-start(bf16[192,2304]{1,0:T(8,128)(2,1)S(1)} %collective-permute-done.107.refs_8_), channel_id=1, source_target_pairs={{8,0},{10,2},{16,8},{18,10},{24,16},{26,18},{28,24},{30,26},{20,28... | collective-permute-start | bytes 2654216 | tf_op jit(solution)/shard_map/ppermute | solution.py:65
  (172 other events, 2129.9 us)
